TPU v7x, 32 devices: a whole 2x2x4 slice. The times are simulated.
32 devices in a mesh: seq: 8 (over z, x), head: 4 (over y, core).
Axes of the slice: x: 2, y: 2, z: 4, core: 2. Of those that a mesh axis runs over, the one named last changes fastest.
Arguments:
- hidden_in: bfloat16 [4, 3072, 1536], P(None, 'seq'), may hold values from -6 to 6
- norm_gain: float32 [1536], replicated, may hold values from 0.5 to 1.5
- proj_gate: bfloat16 [1536, 3072], P(None, 'head'), may hold values from -0.15625 to 0.15625
- proj_inner: bfloat16 [1536, 3072], P(None, 'head'), may hold values from -0.15625 to 0.15625
- proj_step: bfloat16 [1536, 48], P(None, 'head'), may hold values from -0.21875 to 0.21875
- proj_shared: bfloat16 [1536, 256], replicated, may hold values from -0.15625 to 0.15625
- filter_inner: float32 [4, 3072], P(None, 'head'), may hold values from -3 to 3
- filter_inner_bias: float32 [3072], P('head'), may hold values from -1.5 to 1.5
- filter_shared: float32 [4, 256], replicated, may hold values from -3 to 3
- filter_shared_bias: float32 [256], replicated, may hold values from -1.5 to 1.5
- step_bias: float32 [48], P('head'), may hold values from -8 to -3, as said below
- log_rate: float32 [48], P('head'), may hold values from -4 to 1, as said below
- skip_gain: float32 [48], P('head'), may hold values from 0.5 to 2
- gate_gain: float32 [3072], P('head'), may hold values from 0.5 to 1.5
- proj_out: bfloat16 [3072, 1536], P('head'), may hold values from -0.109375 to 0.109375
- cotangent: bfloat16 [4, 3072, 1536], P(None, 'seq', 'head'), may hold values from -6 to 6
Outputs:
- activations: bfloat16 [4, 3072, 1536], P(None, 'seq', 'head')
- grad_input: float32 [4, 3072, 1536], P(None, 'seq', 'head')
- grad_norm_gain: float32 [1536], P('head')
- grad_proj_gate: float32 [1536, 3072], P(None, 'head')
- grad_proj_inner: float32 [1536, 3072], P(None, 'head')
- grad_proj_step: float32 [1536, 48], P(None, 'head')
- grad_proj_shared: float32 [1536, 256], replicated
- grad_filter_inner: float32 [4, 3072], P(None, 'head')
- grad_filter_inner_bias: float32 [3072], P('head')
- grad_filter_shared: float32 [4, 256], replicated
- grad_filter_shared_bias: float32 [256], replicated
- grad_step_bias: float32 [48], P('head')
- grad_log_rate: float32 [48], P('head')
- grad_skip_gain: float32 [48], P('head')
- grad_gate_gain: float32 [3072], P('head')
- grad_proj_out: float32 [3072, 1536], P('head')
Inputs may be any that keep to these rules, and one draw needn't show every extreme that they name: `step_bias`: one value per head. `log_rate`: one value per head.
All inputs are finite; a program needn't handle non-finite values.
Results may differ from a plain program's by a relative error of at most 0.0097.
Values may be sent and summed in bfloat16 or wider, within the bound.
No kernel may reach another device: no remote copies, remote signals or barrier semaphores. Data moves between devices by JAX's collectives and lax.ppermute only.
A program may use at most 320 MiB of HBM per device.

v0:
```python
import jax
import jax.numpy as jnp
from jax import lax
from jax.sharding import PartitionSpec as P

epsilon = 1e-05
highest = lax.Precision.HIGHEST


def passed_along(array, axis, by):
    size = lax.axis_size(axis)
    pairs = [(i, i + by) for i in range(size) if 0 <= i + by < size]
    return lax.ppermute(array, axis, pairs)


def prefix(value, axis, join, neutral, backward):
    count, mine = (lax.axis_size(axis), lax.axis_index(axis))
    pieces = jax.tree.map(lambda part: lax.all_gather(part, axis), value)
    if backward:
        pieces = jax.tree.map(lambda part: part[::-1], pieces)
        mine = count - 1 - mine
    subtotal = jax.tree.map(
        lambda part, zero: jnp.full_like(part, 0) + jnp.asarray(zero, part.dtype), value, neutral
    )

    def lap(position, subtotal):
        longer = join(subtotal, jax.tree.map(lambda part: part[position], pieces))
        return jax.tree.map(lambda new, old: jnp.where(position < mine, new, old), longer, subtotal)

    return lax.fori_loop(0, count - 1, lap, subtotal)


def sigmoid_gated(value):
    return value * jax.nn.sigmoid(value)


def causal_filter(extended, kernel, offset):
    kernel_len = kernel.shape[0]
    length = extended.shape[1] - kernel_len + 1
    summed = offset + kernel[0] * extended[:, 0:length]
    for tap_index in range(1, kernel_len):
        summed = summed + kernel[tap_index] * extended[:, tap_index : tap_index + length]
    return sigmoid_gated(summed)


def decay_terms(step_raw, step_bias, log_rate):
    step_size = jax.nn.softplus(step_raw + step_bias)
    log_decay = jnp.cumsum(-step_size * jnp.exp(log_rate), axis=1)
    return (jnp.swapaxes(step_size, 1, 2), jnp.swapaxes(log_decay, 1, 2))


def block_output(
    inner_heads, step_raw, step_bias, log_rate, shared_b, shared_c, skip_gain, state_in
):
    step_size, log_decay = decay_terms(step_raw, step_bias, log_rate)
    length = inner_heads.shape[1]
    position = jnp.arange(length)
    causal = position[:, None] >= position[None, :]
    log_gap = jnp.where(causal, log_decay[:, :, :, None] - log_decay[:, :, None, :], 0.0)
    weights = jnp.where(causal, jnp.exp(log_gap), 0.0) * step_size[:, :, None, :]
    scores = jnp.einsum("sqn,skn->sqk", shared_c, shared_b, precision=highest)
    mixing = scores[:, None] * weights
    local_out = jnp.einsum("shqk,skhp->sqhp", mixing, inner_heads, precision=highest)
    carried = jnp.einsum(
        "sqn,shpn,shq->sqhp", shared_c, state_in, jnp.exp(log_decay), precision=highest
    )
    return local_out + carried + skip_gain[:, None] * inner_heads


def block_state(inner_heads, step_raw, step_bias, log_rate, shared_b):
    step_size, log_decay = decay_terms(step_raw, step_bias, log_rate)
    final_log = log_decay[:, :, -1:]
    weighting = jnp.exp(final_log - log_decay) * step_size
    state_local = jnp.einsum(
        "shk,skn,skhp->shpn", weighting, shared_b, inner_heads, precision=highest
    )
    return (state_local, jnp.exp(final_log[:, :, 0]))


def block_whole(
    inner_heads, step_raw, step_bias, log_rate, shared_b, shared_c, skip_gain, state_in
):
    output = block_output(
        inner_heads, step_raw, step_bias, log_rate, shared_b, shared_c, skip_gain, state_in
    )
    state_local, block_decay = block_state(inner_heads, step_raw, step_bias, log_rate, shared_b)
    return (output, state_local, block_decay)


def chain_join(earlier, later):
    return (earlier[0] * later[0], later[0][:, :, None, None] * earlier[1] + later[1])


def on_device(
    hidden_in,
    norm_gain,
    proj_gate,
    proj_inner,
    proj_step,
    proj_shared,
    filter_inner,
    filter_inner_bias,
    filter_shared,
    filter_shared_bias,
    step_bias,
    log_rate,
    skip_gain,
    gate_gain,
    proj_out,
    cotangent,
):
    batch_seqs, length, width_d = hidden_in.shape
    local_inner = proj_gate.shape[1]
    local_heads = proj_step.shape[1]
    head_width = local_inner // local_heads
    states = proj_shared.shape[1] // 2
    kernel_len = filter_inner.shape[0]
    rim_len = kernel_len - 1
    full_inner = local_inner * lax.axis_size("head")
    columns = width_d // lax.axis_size("head")
    offset_col = lax.axis_index("head") * columns
    hidden_f = hidden_in.astype(jnp.float32)
    hidden_part = lax.dynamic_slice_in_dim(hidden_f, offset_col, columns, 2)
    inv_rms = lax.rsqrt(jnp.mean(hidden_f * hidden_f, axis=-1, keepdims=True) + epsilon)
    normed = (hidden_f * inv_rms * norm_gain).astype(jnp.bfloat16)
    gate_pre = jnp.dot(normed, proj_gate, preferred_element_type=jnp.float32)
    inner_pre = jnp.dot(normed, proj_inner, preferred_element_type=jnp.float32)
    step_raw = jnp.dot(normed, proj_step, preferred_element_type=jnp.float32)
    shared_pre = jnp.dot(normed, proj_shared, preferred_element_type=jnp.float32)
    left_rims = passed_along(
        (inner_pre[:, length - rim_len :], shared_pre[:, length - rim_len :]), "seq", 1
    )
    ext_inner = jnp.concatenate([left_rims[0], inner_pre], axis=1)
    ext_shared = jnp.concatenate([left_rims[1], shared_pre], axis=1)
    inner_act = causal_filter(ext_inner, filter_inner, filter_inner_bias)
    shared_act = causal_filter(ext_shared, filter_shared, filter_shared_bias)
    inner_heads = inner_act.reshape(batch_seqs, length, local_heads, head_width)
    shared_b = shared_act[..., :states]
    shared_c = shared_act[..., states:]
    state_local, block_decay = block_state(inner_heads, step_raw, step_bias, log_rate, shared_b)
    identity = (jnp.ones((batch_seqs, local_heads), jnp.float32), jnp.zeros_like(state_local))
    state_in = prefix((block_decay, state_local), "seq", chain_join, identity, False)[1]
    ssm_out = block_output(
        inner_heads, step_raw, step_bias, log_rate, shared_b, shared_c, skip_gain, state_in
    ).reshape(batch_seqs, length, local_inner)
    gate_act = sigmoid_gated(gate_pre)
    gated = ssm_out * gate_act
    squares = lax.psum(jnp.sum(gated * gated, axis=-1, keepdims=True), "head")
    gate_rms = lax.rsqrt(squares / full_inner + epsilon)
    mixer_in = (gated * gate_rms * gate_gain).astype(jnp.bfloat16)
    partial_out = jnp.dot(mixer_in, proj_out, preferred_element_type=jnp.float32)
    mixed_part = lax.psum_scatter(partial_out, "head", scatter_dimension=2, tiled=True)
    activations = (hidden_part + mixed_part).astype(jnp.bfloat16)
    cot_full = lax.all_gather(cotangent, "head", axis=2, tiled=True)
    grad_proj_out = jnp.einsum(
        "sqc,sqd->cd", mixer_in, cot_full, preferred_element_type=jnp.float32
    )
    d_mixer = jnp.einsum("sqd,cd->sqc", cot_full, proj_out, preferred_element_type=jnp.float32)
    grad_gate_gain = jnp.sum(d_mixer * gated * gate_rms, axis=(0, 1))
    scaled_mixer = d_mixer * gate_gain
    gate_row = lax.psum(jnp.sum(scaled_mixer * gated, axis=-1, keepdims=True), "head")
    d_gated = (
        gate_rms * scaled_mixer - gated * gate_rms * gate_rms * gate_rms * gate_row / full_inner
    )
    d_ssm = d_gated * gate_act
    sigmoid_z = jax.nn.sigmoid(gate_pre)
    d_gate16 = (d_gated * ssm_out * sigmoid_z * (1.0 + gate_pre * (1.0 - sigmoid_z))).astype(
        jnp.bfloat16
    )
    d_heads = d_ssm.reshape(batch_seqs, length, local_heads, head_width)
    step_size, log_decay = decay_terms(step_raw, step_bias, log_rate)
    local_grad = jnp.einsum(
        "sqhp,shq,sqn->shpn", d_heads, jnp.exp(log_decay), shared_c, precision=highest
    )
    later_grad = prefix((block_decay, local_grad), "seq", chain_join, identity, True)[1]
    d_decay = jnp.sum(later_grad * state_in, axis=(2, 3))
    _, pullback = jax.vjp(
        block_whole,
        inner_heads,
        step_raw,
        step_bias,
        log_rate,
        shared_b,
        shared_c,
        skip_gain,
        state_in,
    )
    block_grads = pullback((d_heads, later_grad, d_decay))
    d_inner_act = block_grads[0].reshape(batch_seqs, length, local_inner)
    d_step16 = block_grads[1].astype(jnp.bfloat16)
    grad_step_bias = block_grads[2]
    grad_log_rate = block_grads[3]
    grad_skip_gain = block_grads[6]
    d_shared_act = lax.psum(jnp.concatenate([block_grads[4], block_grads[5]], axis=-1), "head")
    _, pull_inner = jax.vjp(causal_filter, ext_inner, filter_inner, filter_inner_bias)
    d_ext_inner, grad_filter_inner, grad_filter_inner_bias = pull_inner(d_inner_act)
    _, pull_shared = jax.vjp(causal_filter, ext_shared, filter_shared, filter_shared_bias)
    d_ext_shared, grad_filter_shared, grad_filter_shared_bias = pull_shared(d_shared_act)
    right_edges = (
        passed_along(d_ext_inner[:, :rim_len].astype(jnp.bfloat16), "seq", -1).astype(jnp.float32),
        passed_along(d_ext_shared[:, :rim_len].astype(jnp.bfloat16), "seq", -1).astype(jnp.float32),
    )
    d_inner_body = d_ext_inner[:, rim_len:]
    d_shared_body = d_ext_shared[:, rim_len:]
    d_inner16 = jnp.concatenate(
        [d_inner_body[:, : length - rim_len], d_inner_body[:, length - rim_len :] + right_edges[0]],
        axis=1,
    ).astype(jnp.bfloat16)
    d_shared16 = jnp.concatenate(
        [
            d_shared_body[:, : length - rim_len],
            d_shared_body[:, length - rim_len :] + right_edges[1],
        ],
        axis=1,
    ).astype(jnp.bfloat16)
    grad_proj_gate = jnp.einsum("sqd,sqc->dc", normed, d_gate16, preferred_element_type=jnp.float32)
    grad_proj_inner = jnp.einsum(
        "sqd,sqc->dc", normed, d_inner16, preferred_element_type=jnp.float32
    )
    grad_proj_step = jnp.einsum("sqd,sqc->dc", normed, d_step16, preferred_element_type=jnp.float32)
    grad_proj_shared = jnp.einsum(
        "sqd,sqc->dc", normed, d_shared16, preferred_element_type=jnp.float32
    )
    back_part = jnp.einsum("sqc,dc->sqd", d_gate16, proj_gate, preferred_element_type=jnp.float32)
    back_part = back_part + jnp.einsum(
        "sqc,dc->sqd", d_inner16, proj_inner, preferred_element_type=jnp.float32
    )
    back_part = back_part + jnp.einsum(
        "sqc,dc->sqd", d_step16, proj_step, preferred_element_type=jnp.float32
    )
    d_normed = lax.psum(back_part, "head") + jnp.einsum(
        "sqc,dc->sqd", d_shared16, proj_shared, preferred_element_type=jnp.float32
    )
    scaled_normed = d_normed * norm_gain
    norm_row = jnp.mean(scaled_normed * hidden_f, axis=-1, keepdims=True)
    input_full = inv_rms * scaled_normed - hidden_f * inv_rms * inv_rms * inv_rms * norm_row
    input_grad = lax.dynamic_slice_in_dim(input_full, offset_col, columns, 2)
    gain_full = jnp.sum(d_normed * hidden_f * inv_rms, axis=(0, 1))
    grad_norm_gain = lax.dynamic_slice_in_dim(gain_full, offset_col, columns, 0)
    grad_input = input_grad + cotangent.astype(jnp.float32)
    summed = lax.psum(
        (
            grad_norm_gain,
            grad_proj_gate,
            grad_proj_inner,
            grad_proj_step,
            grad_proj_shared,
            grad_filter_inner,
            grad_filter_inner_bias,
            grad_filter_shared,
            grad_filter_shared_bias,
            grad_step_bias,
            grad_log_rate,
            grad_skip_gain,
            grad_gate_gain,
            grad_proj_out,
        ),
        "seq",
    )
    return (
        activations,
        grad_input,
        summed[0],
        summed[1],
        summed[2],
        summed[3],
        summed[4],
        summed[5],
        summed[6],
        summed[7],
        summed[8],
        summed[9],
        summed[10],
        summed[11],
        summed[12],
        summed[13],
    )


def solution(mesh):
    in_specs = (
        P(None, "seq", None),
        P(),
        P(None, "head"),
        P(None, "head"),
        P(None, "head"),
        P(),
        P(None, "head"),
        P("head"),
        P(),
        P(),
        P("head"),
        P("head"),
        P("head"),
        P("head"),
        P("head", None),
        P(None, "seq", "head"),
    )
    out_specs = (
        P(None, "seq", "head"),
        P(None, "seq", "head"),
        P("head"),
        P(None, "head"),
        P(None, "head"),
        P(None, "head"),
        P(),
        P(None, "head"),
        P("head"),
        P(),
        P(),
        P("head"),
        P("head"),
        P("head"),
        P("head"),
        P("head", None),
    )
    return jax.shard_map(
        on_device, mesh=mesh, in_specs=in_specs, out_specs=out_specs, check_vma=False
    )
```

profile of v0, /device:TPU:0, one launch (start us, length us, event | category | flops | bytes accessed | tf_op | source)
XLA Modules:
  0.0 1518.5 jit_solution(1962225277034620133)
XLA Ops:
  49.6 10.5 fusion.44
  77.9 26.6 %all-gather = f32[32,12,1]{1,2,0:T(1,128)S(1)} all-gather(f32[4,12,1]{1,2,0:T(1,128)S(1)} %bitcast.282), channel_id=2, replica_groups=mesh['seq'=8,'head'=4] {'seq'}, dimensions={0}, use_global_device_ids=true | all-gather | bytes 1728 | tf_op jit(solution)/shard_map/all_gather | solution.py:18
  109.3 141.3 %all-gather.9.cloned.1.call-done = f32[32,12,64,128]{3,2,1,0:T(8,128)} async-done(((f32[4,12,64,128]{3,2,1,0:T(8,128)}), f32[32,12,64,128]{3,2,1,0:T(8,128)}) %all-gather.9.cloned.1.call-update) | async-done | bytes 12582928 | tf_op jit(solution)/shard_map/all_gather | solution.py:18
  250.6 22.9 %while.28 = (s32[]{:T(128)}, f32[4,12,64,128]{3,2,1,0:T(8,128)}, s32[]{:T(128)}, f32[8,4,12]{2,1,0:T(4,128)S(1)}, f32[8,4,12,64,128]{4,3,2,1,0:T(8,128)}, /*index=5*/s32[]{:T(128)}, s32[]{:T(128)}) while((s32[]{:T(128)}, f32[4,12,64,128]{3,2,1,0:T(8,128)}, s32[]{:T(128)}, f32[8,4,12]{2,1,0:T(4,128)S(1)}, ...), condition=%wide.region_4.5_spmd.clone, body=%wide.region_3.4_spmd.clone.sunk | while | flops 1572868 | bytes 4719281 | solution.py:30
  279.6 41.2 %fusion.35 = f32[4,384,12,64]{1,3,2,0:T(8,128)} fusion(f32[4,12,64,384]{3,2,1,0:T(8,128)S(1)} %fusion.96, f32[4,384,12,64]{1,3,2,0:T(8,128)} %bitcast.252, f32[12]{0:T(128)S(1)} %copy-done.84, f32[4,384,12]{1,2,0:T(8,128)S(1)} %copy-done.43, f32[4,12,384]{2,1,0:T(8,128)S(1)} %copy-done.39, f32[4,12,384]{2,1,0:T(8,128)S(1)} %copy-done.42, ...), kind=kOutput, calls=%fused_computation.56 | convolution fusion | flops 5475926016 | bytes 16883760 | tf_op jit(solution)/shard_map/shqk,skhp->sqhp/dot_general | solution.py:63
  327.1 12.2 multiply_reduce_fusion.14
  345.7 11.5 multiply_reduce_fusion.7
  363.3 13.9 multiply_reduce_fusion.8
  407.8 44.5 %fusion.15 = (f32[4,12,384]{2,1,0:T(8,128)S(1)}, f32[4,12,384]{2,1,0:T(8,128)S(1)}, f32[4,12,384]{2,1,0:T(8,128)S(1)}, f32[4,384,384]{2,1,0:T(8,128)}) fusion(f32[4,12,384]{2,1,0:T(8,128)S(1)} %copy.304, f32[4,12,384]{2,1,0:T(8,128)S(1)} %copy-done.41, f32[4,384,384]{2,1,0:T(8,128)S(1)} %copy-done.31, pred[384,384]{1,0:T(8,128)(4,1)S(1)} %copy-done.37, ...), kind=kOutput, calls=%fused_computation.22 | convolution fusion | flops 5541341184 | bytes 14671872 | tf_op jit(solution)/shard_map/transpose(jvp(shqk,skhp->sqhp))/dot_general | solution.py:63
  452.4 15.1 reduce-window.36
  477.1 9.5 fusion.77
  496.4 68.9 %all-gather.11.cloned.1.call-done = f32[32,12,64,128]{3,2,1,0:T(8,128)} async-done(((f32[4,12,64,128]{3,2,1,0:T(8,128)}), f32[32,12,64,128]{3,2,1,0:T(8,128)}) %all-gather.11.cloned.1.call-update) | async-done | bytes 12582928 | tf_op jit(solution)/shard_map/all_gather | solution.py:18
  565.2 11.8 rev.7
  577.0 22.8 %while.29 = (s32[]{:T(128)}, f32[4,12,64,128]{3,2,1,0:T(8,128)}, s32[]{:T(128)}, f32[8,4,12]{2,1,0:T(4,128)S(1)}, f32[8,4,12,64,128]{4,3,2,1,0:T(8,128)}, /*index=5*/s32[]{:T(128)}, s32[]{:T(128)}) while((s32[]{:T(128)}, f32[4,12,64,128]{3,2,1,0:T(8,128)}, s32[]{:T(128)}, f32[8,4,12]{2,1,0:T(4,128)S(1)}, ...), condition=%wide.region_11.12_spmd.clone, body=%wide.region_10.11_spmd.clone.sunk | while | flops 1572868 | bytes 4719281 | solution.py:30
  616.1 15.1 reduce-window.34
  632.9 29.0 %bitcast_add_fusion.2 = f32[4,384,12,64]{1,3,2,0:T(8,128)} fusion(f32[4,384,12,64]{1,3,2,0:T(8,128)} %bitcast.246, f32[4,384,12,64]{1,3,2,0:T(8,128)} %copy-done.11, f32[4,384,12]{1,2,0:T(8,128)S(1)} %copy.301, f32[12]{0:T(128)S(1)} %copy-done.84, f32[4,12,64,384]{3,2,1,0:T(8,128)} %bitcast.247, f32[4,12,384]{2,1,0:T(8,128)S(1)} %copy.304, ...), kind=kOutput, calls=%fused_computation.53 | convolution fusion | flops 5475926016 | bytes 21602352 | tf_op jit(solution)/shard_map/transpose(jvp(shqk,skhp->sqhp))/dot_general | solution.py:63
  676.9 11.8 multiply_reduce_fusion.11
  695.7 9.6 fusion.147
  748.0 9.9 convolution_bitcast_fusion
  762.4 160.8 %all-reduce.25.cloned.1.call-done = (f32[4,384,1536]{2,1,0:T(8,128)}, f32[4,384,256]{2,1,0:T(8,128)}) async-done(((f32[4,384,1536]{2,1,0:T(8,128)}, f32[4,384,256]{2,1,0:T(8,128)}), (f32[4,384,1536]{2,1,0:T(8,128)}, f32[4,384,256]{2,1,0:T(8,128)})) %all-reduce.25.cloned.1.call-update) | async-done | bytes 11010064 | tf_op jit(solution)/shard_map/psum | solution.py:231
  947.4 56.9 %reduce-scatter.2.cloned.1.call-done = f32[4,384,384]{2,1,0:T(8,128)} async-done(((f32[4,384,1536]{2,1,0:T(8,128)}), f32[4,384,384]{2,1,0:T(8,128)}) %reduce-scatter.2.cloned.1.call-update) | async-done | bytes 2359312 | tf_op jit(solution)/shard_map/reduce_scatter | solution.py:152
  1008.0 11.9 multiply_reduce_fusion.2
  1020.0 39.7 %all-reduce.17 = (f32[384]{0:T(512)}, f32[4,768]{1,0:T(4,128)}, f32[768]{0:T(1024)}, f32[4,256]{1,0:T(4,128)}, f32[256]{0:T(256)}, /*index=5*/f32[12]{0:T(128)}, f32[12]{0:T(128)}, f32[12]{0:T(128)}, f32[768]{0:T(1024)}) all-reduce(f32[384]{0:T(512)S(1)} %dynamic_slice.39, ...), channel_id=1, replica_groups=mesh['seq'=8,'head'=4] {'seq'}, use_global_device_ids=true, to_apply=%region_28.30 | all-reduce | flops 6308 | bytes 50464 | tf_op jit(solution)/shard_map/psum | solution.py:241
  1064.2 435.0 %all-reduce.23.cloned.1.call-done = (f32[1536,768]{1,0:T(8,128)}, f32[1536,768]{1,0:T(8,128)}, f32[1536,12]{0,1:T(8,128)}, f32[1536,256]{1,0:T(8,128)}, f32[768,1536]{1,0:T(8,128)}) async-done(((f32[1536,768]{1,0:T(8,128)}, f32[1536,768]{1,0:T(8,128)}, f32[1536,12]{0,1:T(8,128)}, f32[1536,256]{1,0:T(8,128)}, f32[768,1536]{1,0:T(8,128)}), (f32[1536,768]{1,0:T(8,128)}, f32[1536,768]{1,0:T(8,128)}, ...) | async-done | bytes 15802384 | tf_op jit(solution)/shard_map/psum | solution.py:241
  (379 shorter events, 315.9 us)
Async XLA Ops:
  7.2 319.9 %copy-start = (bf16[1536,768]{1,0:T(8,128)(2,1)S(1)}, bf16[1536,768]{1,0:T(8,128)(2,1)}, u32[]{:S(2)}) copy-start(bf16[1536,768]{1,0:T(8,128)(2,1)} %param.23) | copy-start | bytes 7077892
  7.2 243.4 %all-gather.9.cloned.1.call-start = ((), (), s32[]{:S(2)}) async-start(), calls=%async_computation.3 | async-start | bytes 14155776 | tf_op jit(solution)/shard_map/all_gather | solution.py:18
  11.1 316.0 %copy-start.46 = (f32[4,384]{1,0:T(4,128)}, f32[4,384]{1,0:T(4,128)S(1)}, u32[]{:S(2)}) copy-start(f32[4,384]{1,0:T(4,128)S(1)} %add_rsqrt_fusion) | copy-start | bytes 18436
  15.2 28.3 %collective-permute-start.1 = (f32[4,3,256]{2,1,0:T(4,128)S(1)}, f32[4,3,256]{2,1,0:T(4,128)S(1)}, u32[]{:S(2)}, u32[]{:S(2)}) collective-permute-start(f32[4,3,256]{2,1,0:T(4,128)S(1)} %slice.165), channel_id=1, source_target_pairs={{0,4},{4,8},{8,12},{12,16},{16,20},{20,24},{24,28},{1,5},{5,9},{9,... | collective-permute-start | bytes 36872 | tf_op jit(solution)/shard_map/ppermute | solution.py:13
  24.2 25.4 %collective-permute-start = (f32[4,3,768]{2,1,0:T(4,128)S(1)}, f32[4,3,768]{2,1,0:T(4,128)S(1)}, u32[]{:S(2)}, u32[]{:S(2)}) collective-permute-start(f32[4,3,768]{2,1,0:T(4,128)S(1)} %slice.160), channel_id=1, source_target_pairs={{0,4},{4,8},{8,12},{12,16},{16,20},{20,24},{24,28},{1,5},{5,9},{9,... | collective-permute-start | bytes 110600 | tf_op jit(solution)/shard_map/ppermute | solution.py:13
  30.1 360.5 %copy-start.7 = (f32[4,384,12]{2,0,1:T(4,128)}, f32[4,384,12]{2,0,1:T(4,128)S(1)}, u32[]{:S(2)}) copy-start(f32[4,384,12]{2,0,1:T(4,128)S(1)} %copy.276) | copy-start | bytes 221188
  73.6 272.1 %all-gather.7.cloned.1.call-start = ((), (), s32[]{:S(2)}) async-start(), calls=%async_computation.2 | async-start | bytes 5898240 | tf_op jit(solution)/shard_map/all_gather | solution.py:154
  74.4 490.8 %all-gather.11.cloned.1.call-start = ((), (), s32[]{:S(2)}) async-start(), calls=%async_computation.4 | async-start | bytes 14155776 | tf_op jit(solution)/shard_map/all_gather | solution.py:18
  74.5 205.0 %copy-start.36 = (pred[384,384]{1,0:T(8,128)(4,1)}, pred[384,384]{1,0:T(8,128)(4,1)S(1)}, u32[]{:S(2)}) copy-start(pred[384,384]{1,0:T(8,128)(4,1)S(1)} %iota_compare_fusion) | copy-start | bytes 442372
  390.5 532.6 %all-reduce.25.cloned.1.call-start = ((), (), s32[]{:S(2)}) async-start(), calls=%async_computation.6 | async-start | bytes 22020096 | tf_op jit(solution)/shard_map/psum | solution.py:231
  705.4 9.5 collective-permute-start.2
  727.1 277.1 %reduce-scatter.2.cloned.1.call-start = ((), (), s32[]{:S(2)}) async-start(), calls=%async_computation.1 | async-start | bytes 11796480 | tf_op jit(solution)/shard_map/reduce_scatter | solution.py:152
  737.5 761.7 %all-reduce.23.cloned.1.call-start = ((), (), s32[]{:S(2)}) async-start(), calls=%async_computation.5 | async-start | bytes 31653888 | tf_op jit(solution)/shard_map/psum | solution.py:241
  757.9 165.3 %copy-start.18 = (f32[4,384,256]{2,1,0:T(8,128)S(1)}, f32[4,384,256]{2,1,0:T(8,128)}, u32[]{:S(2)}) copy-start(f32[4,384,256]{2,1,0:T(8,128)} %copy-done.17) | copy-start | bytes 4718596
  757.9 165.3 %copy-start.45 = (f32[4,3,256]{2,1,0:T(4,128)S(1)}, f32[4,3,256]{2,1,0:T(4,128)}, u32[]{:S(2)}) copy-start(f32[4,3,256]{2,1,0:T(4,128)} %copy-done.44) | copy-start | bytes 36868
  762.4 163.5 %copy-start.61 = (f32[1,256]{1,0:T(1,128)S(1)}, f32[1,256]{1,0:T(1,128)}, u32[]{:S(2)}) copy-start(f32[1,256]{1,0:T(1,128)} %copy-done.60) | copy-start | bytes 3076
  762.4 163.6 %copy-start.63 = (f32[1,256]{1,0:T(1,128)S(1)}, f32[1,256]{1,0:T(1,128)}, u32[]{:S(2)}) copy-start(f32[1,256]{1,0:T(1,128)} %copy-done.62) | copy-start | bytes 3076
  762.4 163.6 %copy-start.65 = (f32[1,256]{1,0:T(1,128)S(1)}, f32[1,256]{1,0:T(1,128)}, u32[]{:S(2)}) copy-start(f32[1,256]{1,0:T(1,128)} %copy-done.64) | copy-start | bytes 3076
  762.4 163.6 %copy-start.67 = (f32[1,256]{1,0:T(1,128)S(1)}, f32[1,256]{1,0:T(1,128)}, u32[]{:S(2)}) copy-start(f32[1,256]{1,0:T(1,128)} %copy-done.66) | copy-start | bytes 3076
  927.0 8.8 collective-permute-start.3
  947.1 60.8 %copy-start.78 = (f32[12]{0:T(128)S(1)}, f32[12]{0:T(128)}, u32[]{:S(2)}) copy-start(f32[12]{0:T(128)} %get-tuple-element.336) | copy-start | bytes 148
  947.1 60.8 %copy-start.79 = (f32[12]{0:T(128)S(1)}, f32[12]{0:T(128)}, u32[]{:S(2)}) copy-start(f32[12]{0:T(128)} %get-tuple-element.338) | copy-start | bytes 148
  947.1 60.8 %copy-start.81 = (f32[12]{0:T(128)S(1)}, f32[12]{0:T(128)}, u32[]{:S(2)}) copy-start(f32[12]{0:T(128)} %param.32) | copy-start | bytes 148
  947.1 60.8 %copy-start.33 = (bf16[1536,256]{1,0:T(8,128)(2,1)S(1)}, bf16[1536,256]{1,0:T(8,128)(2,1)}, u32[]{:S(2)}) copy-start(bf16[1536,256]{1,0:T(8,128)(2,1)} %param.26) | copy-start | bytes 2359300
  (82 other events, 899.5 us)
Sparse Core Ops, SparseCore 0:
  73.7 176.8 all-gather.8
  252.2 35.5 all-gather.6
  390.7 174.5 all-gather.10
  727.2 195.8 all-reduce.24
  925.6 78.5 reduce-scatter.1
  1010.4 488.8 all-reduce.22
where the time goes:
time: 1520 us
  waiting for transfers between devices  864 us (57%)
  matrix products  277 us (18%)
  other arithmetic  192 us (13%)
  local copies, waits for them, and re-layouts  79.1 us (5%)
  blocking collectives  78.7 us (5%)
  between operations  15.8 us (1%)
    psum x1, waiting for transfers between devices, on_device(): lax.psum((grad_norm_gain, grad_proj_gate, grad_proj_inner, grad_proj_step...  435 us
    all_gather x2, waiting for transfers between devices, prefix(): pieces = jax.tree.map(lambda part: lax.all_gather(part, axis), value)  210 us
    psum x1, waiting for transfers between devices, on_device(): lax.psum(back_part, 'head')  161 us
    dot_general x3, matrix products, block_output(): jnp.einsum('shqk,skhp->sqhp', mixing, inner_heads, precision=highest)  115 us
    reduce_scatter x1, waiting for transfers between devices, on_device(): lax.psum_scatter(partial_out, 'head', scatter_dimension=2, tiled=True)  56.9 us
    another operation x16, other arithmetic  48.5 us
    select_n x14, other arithmetic, lap(): jnp.where(position < mine, new, old)  45.7 us
    psum x1, blocking collectives, on_device(): lax.psum((grad_norm_gain, grad_proj_gate, grad_proj_inner, grad_proj_step...  39.7 us
  transfers between devices with their start and end apart: 10, of which 5 were waited for; matrix products, arithmetic and copies ran while one was open for 20% of the time, Pallas kernels for 0%

commit v1 on v0

v1 whole, which is shorter than its diff:
```python
import functools

import jax
import jax.numpy as jnp
import numpy as np
from jax import lax
from jax.experimental import pallas as pl
from jax.experimental.pallas import tpu as pltpu
from jax.sharding import PartitionSpec as P

epsilon = 1e-05
lanes = 128
chunk = 128
rim = 16
f32 = jnp.float32
bf16 = jnp.bfloat16
vmem_limit = 56 * 1024 * 1024


def nn(left, right):
    return jnp.dot(left, right, preferred_element_type=f32)


def nt(left, right):
    return lax.dot_general(left, right, (((1,), (1,)), ((), ())), preferred_element_type=f32)


def tn(left, right):
    return lax.dot_general(left, right, (((0,), (0,)), ((), ())), preferred_element_type=f32)


def two_parts(value):
    high = value.astype(bf16)
    return jnp.concatenate([high, (value - high.astype(f32)).astype(bf16)], axis=1)


def three_parts(value):
    high = value.astype(bf16)
    rest = value - high.astype(f32)
    middle = rest.astype(bf16)
    low = (rest - middle.astype(f32)).astype(bf16)
    return jnp.concatenate([high, middle, low], axis=1)


def summed_by(triangle, value):
    parts = nn(triangle, three_parts(value))
    return parts[:, :lanes] + parts[:, lanes : 2 * lanes] + parts[:, 2 * lanes :]


def iota(shape, dim):
    return lax.broadcasted_iota(jnp.int32, shape, dim)


def triangle_of(kind):
    row, col = iota((chunk, chunk), 0), iota((chunk, chunk), 1)
    keep = {"upto": row >= col, "from": row <= col, "before": row > col}[kind]
    return jnp.where(keep, 1.0, 0.0).astype(bf16)


def sigmoid(value):
    return 0.5 * jnp.tanh(0.5 * value) + 0.5


def softplus(value):
    return jnp.maximum(value, 0.0) + jnp.log1p(jnp.exp(-jnp.abs(value)))


def whole(shape):
    return pl.BlockSpec(shape, lambda s: (0,) * len(shape))


def per_seq(*dims, first=0):
    return pl.BlockSpec((None,) + dims, lambda s: (s + first,) + (0,) * len(dims))


def grid_call(kernel, seqs, in_specs, out_specs, out_shape, scratch, cost, into=()):
    given = len(in_specs)

    def filling(*refs):
        kernel(*refs[:given], *refs[given + len(into) :])

    call = pl.pallas_call(
        filling,
        grid=(seqs,),
        in_specs=in_specs + [pl.BlockSpec(memory_space=pl.ANY)] * len(into),
        input_output_aliases={given + at: at for at in range(len(into))},
        out_specs=out_specs,
        out_shape=out_shape,
        scratch_shapes=scratch,
        compiler_params=pltpu.CompilerParams(
            vmem_limit_bytes=vmem_limit, dimension_semantics=("arbitrary",)
        ),
        cost_estimate=pl.CostEstimate(flops=cost, bytes_accessed=cost, transcendentals=0),
    )
    return lambda *operands: call(*operands, *into)


def cheap(width):
    return pltpu.CompilerParams(vmem_limit_bytes=vmem_limit, dimension_semantics=("arbitrary",)), (
        pl.CostEstimate(flops=width, bytes_accessed=width, transcendentals=0)
    )


def product_kernel(at_ref, left_ref, right_ref, out_ref, *, dot):
    out_ref[...] = dot(left_ref[...], right_ref[...]).astype(out_ref.dtype)


def product(dot, left, right, dtype, start=0, rows=None):
    depth, total = left.shape if dot is tn else left.shape[::-1]
    rows = total if rows is None else rows
    size = rows // 2 if rows % 256 == 0 else rows
    cols = right.shape[0] if dot is nt else right.shape[1]
    if dot is tn:
        left_spec = pl.BlockSpec((depth, size), lambda i, at: (0, at[0] + i))
    else:
        left_spec = pl.BlockSpec((size, depth), lambda i, at: (at[0] + i, 0))
    params, cost = cheap(10**5)
    return pl.pallas_call(
        functools.partial(product_kernel, dot=dot),
        grid_spec=pltpu.PrefetchScalarGridSpec(
            num_scalar_prefetch=1,
            grid=(rows // size,),
            in_specs=[left_spec, pl.BlockSpec(right.shape, lambda i, at: (0, 0))],
            out_specs=pl.BlockSpec((size, cols), lambda i, at: (i, 0)),
        ),
        out_shape=jax.ShapeDtypeStruct((rows, cols), dtype),
        compiler_params=params,
        cost_estimate=cost,
    )(jnp.asarray(start // size, jnp.int32).reshape(1), left, right)


def back_kernel(
    blocks_ref, gate_ref, inner_ref, raw_ref, *refs, parts,
):
    weight_refs, out_ref, buffers = refs[: 3 * parts], refs[3 * parts], refs[3 * parts + 1 :]
    size = weight_refs[0].shape[0]

    @pl.when(pl.program_id(0) == 0)
    def _():
        for part in range(parts):
            rows = slice(part * size, (part + 1) * size)
            buffers[0][rows, :] = weight_refs[part][...]
            buffers[1][rows, :] = weight_refs[parts + part][...]
            buffers[2][:, rows] = weight_refs[2 * parts + part][...]

    out = nt(gate_ref[...], buffers[0][...]) + nt(inner_ref[...], buffers[1][...])
    out = out + nn(raw_ref[:, : buffers[2].shape[0]], buffers[2][...])
    out_ref[...] = out.astype(out_ref.dtype)


def back_product(blocks, size, gate, inner, raw, gate_w, inner_w, step_w, dtype):
    seqs, length, width = gate.shape
    parts = blocks.shape[0]

    def at_seq(array):
        return pl.BlockSpec((None, length, array.shape[2]), lambda s, at: (s, 0, 0))

    rows = [
        pl.BlockSpec((size, width), lambda s, at, part=part: (at[part], 0))
        for part in range(parts)
    ]
    cols = [
        pl.BlockSpec((step_w.shape[0], size), lambda s, at, part=part: (0, at[part]))
        for part in range(parts)
    ]
    params, cost = cheap(10**5)
    return pl.pallas_call(
        functools.partial(back_kernel, parts=parts),
        grid_spec=pltpu.PrefetchScalarGridSpec(
            num_scalar_prefetch=1,
            grid=(seqs,),
            in_specs=[at_seq(gate), at_seq(inner), at_seq(raw)] + rows + rows + cols,
            out_specs=pl.BlockSpec((length, parts * size), lambda s, at: (s, 0)),
            scratch_shapes=[
                pltpu.VMEM((parts * size, width), bf16),
                pltpu.VMEM((parts * size, width), bf16),
                pltpu.VMEM((step_w.shape[0], parts * size), bf16),
            ],
        ),
        out_shape=jax.ShapeDtypeStruct((seqs * length, parts * size), dtype),
        compiler_params=params,
        cost_estimate=cost,
    )(blocks, gate, inner, raw, *[gate_w] * parts, *[inner_w] * parts, *[step_w] * parts)


def spans(total, width):
    return [slice(at, at + width) for at in range(0, total, width)]


def project_kernel(
    hidden_ref, gain_ref, inner_w_ref, shared_w_ref, step_w_ref,
    normed_ref, inner_ref, shared_ref, raw_ref, inv_ref, rim_inner_ref, rim_shared_ref,
):
    length = hidden_ref.shape[0]
    heads = step_w_ref.shape[0]
    for rows in spans(length, chunk):
        hidden = hidden_ref[rows, :].astype(f32)
        inv = lax.rsqrt(jnp.mean(hidden * hidden, axis=1, keepdims=True) + epsilon)
        normed_ref[rows, :] = (hidden * inv * gain_ref[...]).astype(bf16)
        inv_ref[rows, :] = jnp.broadcast_to(inv, (chunk, lanes))
    normed = normed_ref[...]
    inner_ref[...] = nn(normed, inner_w_ref[...])
    shared_ref[...] = nn(normed, shared_w_ref[...])
    raw_ref[...] = jnp.zeros((length, lanes), f32)
    raw_ref[:, :heads] = nt(normed, step_w_ref[...])
    rim_inner_ref[...] = inner_ref[length - rim :, :]
    rim_shared_ref[...] = shared_ref[length - rim :, :]


def filter_forward(buffer, taps_ref, bias_ref, start, column, taps):
    summed = bias_ref[0:1, column]
    for tap in range(taps):
        summed = summed + taps_ref[tap : tap + 1, column] * buffer[
            pl.ds(rim + start - taps + 1 + tap, chunk), column
        ]
    s = sigmoid(summed)
    return summed * s, s * (1.0 + summed * (1.0 - s))


def states_kernel(
    inner_ref, rim_inner_ref, shared_ref, rim_shared_ref, raw_ref,
    taps_ref, bias_ref, taps_s_ref, bias_s_ref, step_bias_ref, rate_ref, spread_ref,
    x_ref, slope_ref, shared_act_ref, slope_s_ref, step_ref, decay_ref, decay_t_ref, local_ref,
    total_ref, state_ref,
    inner_buf, shared_buf, act_buf,
    *, taps, states,
):
    length, width = inner_ref.shape
    inner_buf[0:rim, :] = rim_inner_ref[...]
    inner_buf[rim:, :] = inner_ref[...]
    shared_buf[0:rim, :] = rim_shared_ref[...]
    shared_buf[rim:, :] = shared_ref[...]
    upto = triangle_of("upto")
    spread = spread_ref[...]
    base = jnp.zeros((1, lanes), f32)
    state = jnp.zeros((states, width), f32)
    for index, rows in enumerate(spans(length, chunk)):
        for column in spans(width, lanes):
            value, slope = filter_forward(
                inner_buf, taps_ref, bias_ref, rows.start, column, taps
            )
            x_ref[rows, column] = value
            slope_ref[rows, column] = slope.astype(bf16)
        for column in spans(2 * states, lanes):
            value, slope = filter_forward(
                shared_buf, taps_s_ref, bias_s_ref, rows.start, column, taps
            )
            shared_act_ref[rows, column] = value.astype(bf16)
            slope_s_ref[rows, column] = slope
        step = softplus(raw_ref[rows, :] + step_bias_ref[...])
        local = summed_by(upto, step * rate_ref[...])
        last = local[chunk - 1 : chunk, :]
        step_ref[rows, :] = step
        decay = local + base
        decay_ref[rows, :] = decay
        decay_t_ref[:, rows] = jnp.transpose(decay)[:16, :]
        weight = nn(two_parts(jnp.exp(last - local) * step), spread)
        act_buf[...] = (weight * x_ref[rows, :]).astype(bf16)
        local_ref[index, :, :] = state.astype(bf16)
        kept = nn(two_parts(jnp.broadcast_to(jnp.exp(last), (8, lanes))), spread)[0:1, :]
        state = kept * state + tn(shared_act_ref[rows, 0:states], act_buf[...])
        base = base + last
    state_ref[...] = state.astype(bf16)
    total_ref[...] = jnp.broadcast_to(base, (8, lanes))


def pair_masks():
    low = iota((chunk, lanes), 1) < lanes // 2
    return low, jnp.logical_not(low)


def halves(value, masks):
    zero = jnp.zeros_like(value)
    return jnp.concatenate(
        [jnp.where(masks[0], value, zero), jnp.where(masks[1], value, zero)], axis=0
    )


def fade(decay, decay_t, head, causal):
    gap = decay[:, head : head + 1] - decay_t[head : head + 1, :]
    return jnp.exp(jnp.where(causal, gap, -1e30))


def mix_kernel(
    x_ref, shared_act_ref, step_ref, decay_ref, decay_t_ref, local_ref, skip_ref, spread_ref,
    out_ref,
    *, states,
):
    length, width = x_ref.shape
    causal = iota((chunk, chunk), 0) >= iota((chunk, chunk), 1)
    masks = pair_masks()
    spread = spread_ref[...]
    base = jnp.zeros((1, lanes), f32)
    for index, rows in enumerate(spans(length, chunk)):
        b, c = shared_act_ref[rows, 0:states], shared_act_ref[rows, states:]
        scores = nt(c, b)
        x = x_ref[rows, :]
        decay = decay_ref[rows, :]
        decay_t = decay_t_ref[:, rows]
        stepped = (x * nn(two_parts(step_ref[rows, :]), spread)).astype(bf16)
        out = skip_ref[...] * x
        if index > 0:
            out = out + nn(two_parts(jnp.exp(decay - base)), spread) * nn(c, local_ref[index])
        base = decay[chunk - 1 : chunk, :]
        for pair, column in enumerate(spans(width, lanes)):
            mixing = jnp.concatenate(
                [
                    (fade(decay, decay_t, 2 * pair + side, causal) * scores).astype(bf16)
                    for side in range(2)
                ],
                axis=1,
            )
            part = nn(mixing, halves(stepped[:, column], masks))
            out_ref[rows, column] = out[:, column] + part


def gate_kernel(
    local_out_ref, shared_act_ref, decay_ref, state_in_ref, gate_ref, mixer_grad_ref, gain_ref,
    spread_ref,
    out_ref, sums_ref,
    square_buf, product_buf,
    *, states,
):
    length, width = local_out_ref.shape
    spread = spread_ref[...]
    for rows in spans(length, chunk):
        faded = nn(two_parts(jnp.exp(decay_ref[rows, :])), spread)
        out = local_out_ref[rows, :] + faded * nn(
            shared_act_ref[rows, states:], state_in_ref[...]
        )
        out_ref[rows, :] = out
        gate = gate_ref[rows, :]
        gated = out * gate * sigmoid(gate)
        square_buf[rows, :] = (gated * gated).astype(bf16)
        product_buf[rows, :] = (
            gated * mixer_grad_ref[rows, :] * gain_ref[...]
        ).astype(bf16)
    ones = jnp.ones((8, width), bf16)
    first = nt(ones, square_buf[...])
    second = nt(ones, product_buf[...])
    sums_ref[...] = jnp.where(iota((8, length), 0) < 4, first, second)


def gate_back_kernel(
    out_ref, gate_ref, mixer_grad_ref, sums_ref, gain_ref, shared_act_ref, decay_ref, spread_ref,
    mixer_in_ref, d_gate_ref, d_ssm_ref, lam_ref, gain_grad_ref,
    *, states, full,
):
    length, width = out_ref.shape
    spread = spread_ref[...]
    gain = gain_ref[...]
    summed = jnp.sum(sums_ref[...], axis=0)
    square = summed[0:1, :] * (1.0 / full)
    product = summed[4:5, :] * (1.0 / full)
    rms = lax.rsqrt(square + epsilon)
    scalars = jnp.concatenate([rms, rms * rms * rms * product, jnp.zeros((6, length), f32)], axis=0)
    gain_grad = jnp.zeros((1, width), f32)
    lam = jnp.zeros((states, width), f32)
    for rows in spans(length, chunk):
        columns = jnp.transpose(scalars[:, rows])
        rms_c, row_c = columns[:, 0:1], columns[:, 1:2]
        out = out_ref[rows, :]
        gate = gate_ref[rows, :]
        mixer_grad = mixer_grad_ref[rows, :]
        s = sigmoid(gate)
        act = gate * s
        gated = out * act
        normal = gated * rms_c
        mixer_in_ref[rows, :] = (normal * gain).astype(bf16)
        gain_grad = gain_grad + jnp.sum(mixer_grad * normal, axis=0, keepdims=True)
        d_gated = rms_c * (mixer_grad * gain) - gated * row_c
        d_ssm = d_gated * act
        d_ssm_ref[rows, :] = d_ssm
        d_gate_ref[rows, :] = (d_gated * out * s * (1.0 + gate * (1.0 - s))).astype(bf16)
        faded = nn(two_parts(jnp.exp(decay_ref[rows, :])), spread)
        lam = lam + tn(shared_act_ref[rows, states:], (faded * d_ssm).astype(bf16))
    lam_ref[...] = lam.astype(bf16)
    gain_grad_ref[...] = jnp.broadcast_to(gain_grad, (8, width))


def mix_back_kernel(
    x_ref, shared_act_ref, step_ref, decay_ref, decay_t_ref, local_ref, state_in_ref, d_ssm_ref,
    spread_ref, gather_ref,
    d_x_ref, d_shared_ref, d_decay_ref,
    column_buf,
    *, states,
):
    length, width = x_ref.shape
    causal = iota((chunk, chunk), 0) >= iota((chunk, chunk), 1)
    masks = pair_masks()
    spread, gather = spread_ref[...], gather_ref[...]
    since, before = triangle_of("from"), triangle_of("before")
    lam = jnp.zeros((states, width), f32)
    heads_here = 2 * (width // lanes)
    column_buf[...] = jnp.zeros_like(column_buf)
    row_at, col_at = iota((2 * chunk, lanes), 0), iota((2 * chunk, lanes), 1)
    all_rows = spans(length, chunk)
    for index in reversed(range(len(all_rows))):
        rows = all_rows[index]
        b, c = shared_act_ref[rows, 0:states], shared_act_ref[rows, states:]
        xf = x_ref[rows, :]
        d_out = d_ssm_ref[rows, :]
        decay = decay_ref[rows, :]
        decay_t = decay_t_ref[:, rows]
        step = step_ref[rows, :]
        if index > 0:
            base = decay_ref[rows.start - 1 : rows.start, :]
        else:
            base = jnp.zeros((1, lanes), f32)
        last = decay[chunk - 1 : chunk, :]
        heads = jnp.concatenate([jnp.exp(base), jnp.exp(last - base), jnp.zeros((6, lanes), f32)])
        heads = nn(two_parts(heads), spread)
        entered = local_ref[index].astype(f32) + heads[0:1, :] * state_in_ref[...].astype(f32)
        entered16 = entered.astype(bf16)
        lam16 = lam.astype(bf16)
        scores = nt(c, b)
        faded = nn(two_parts(jnp.exp(decay - base)), spread)
        fading = nn(two_parts(jnp.exp(last - decay)), spread)
        steps = nn(two_parts(step), spread)
        stepped = (xf * steps).astype(bf16)
        d_faded = (faded * d_out).astype(bf16)
        x_faded = (fading * steps * xf).astype(bf16)
        d_c = nt(d_faded, entered16)
        d_b = nt(x_faded, lam16)
        carried = nn(c, entered16)
        carrying = nn(b, lam16)
        queries = nn((d_faded.astype(f32) * carried).astype(bf16), gather)
        keys = nn((x_faded.astype(f32) * carrying).astype(bf16), gather)
        across = jnp.sum(lam * entered, axis=0, keepdims=True) * heads[1:2, :]
        across = nn(jnp.broadcast_to(across, (8, width)).astype(bf16), gather)[0:1, :]
        d_x = fading * carrying
        d_scores = jnp.zeros((chunk, chunk), f32)
        for pair, column in enumerate(spans(width, lanes)):
            d_stack = halves(d_out[:, column].astype(bf16), masks)
            d_mixing = nt(d_stack, stepped[:, column])
            mixed, grads = [], []
            for side in range(2):
                head = 2 * pair + side
                faint = fade(decay, decay_t, head, causal)
                d_score = faint * d_mixing[side * chunk : (side + 1) * chunk, :]
                d_scores = d_scores + d_score
                mixed.append((faint * scores).astype(bf16))
                grad = (d_score * scores).astype(bf16)
                grads.append(grad)
                column_buf[head : head + 1, :] = jnp.sum(
                    grad.astype(f32), axis=0, keepdims=True
                )
            code = jnp.where(col_at == 2 * pair + row_at // chunk, 1.0, 0.0).astype(bf16)
            queries = queries + nn(jnp.concatenate(grads, axis=1), code)
            part = tn(jnp.concatenate(mixed, axis=0), d_stack)
            d_x_ref[rows, column] = d_x[:, column] + part
        queries = queries - jnp.transpose(column_buf[...])
        d_decay_ref[rows, :] = summed_by(since, queries) + summed_by(before, keys) + across
        d_scores16 = d_scores.astype(bf16)
        d_shared_ref[rows, 0:states] = d_b + tn(d_scores16, c)
        d_shared_ref[rows, states:] = d_c + nn(d_scores16, b)
        lam = heads[1:2, :] * lam + tn(c, d_faded)


def filter_backward(buffer, taps_ref, start, size, column, taps):
    total = None
    for tap in range(taps):
        term = taps_ref[tap : tap + 1, column] * buffer[
            pl.ds(rim + start + taps - 1 - tap, size), column
        ]
        total = term if total is None else total + term
    return total


def filter_adjoint(buffer, inner_buf, taps_ref, length, width, taps, body_ref, edge_ref, tail_ref,
                   taps_grad_ref):
    for column in spans(width, lanes):
        edge_ref[:, column] = filter_backward(buffer, taps_ref, -rim, rim, column, taps).astype(
            bf16
        )
        rows_grad = [jnp.zeros((8, lanes), f32) for _ in range(taps + 1)]
        for rows in spans(length, chunk):
            body = filter_backward(buffer, taps_ref, rows.start, chunk, column, taps)
            body_ref[rows, column] = body.astype(bf16)
            if rows.stop == length:
                tail_ref[:, column] = body[chunk - rim :, :]
            grad = buffer[pl.ds(rim + rows.start, chunk), column]
            for tap in range(taps):
                moved = inner_buf[pl.ds(rim + rows.start - taps + 1 + tap, chunk), column]
                rows_grad[tap] = rows_grad[tap] + jnp.sum(
                    (grad * moved).reshape(chunk // 8, 8, lanes), axis=0
                )
            rows_grad[taps] = rows_grad[taps] + jnp.sum(
                grad.reshape(chunk // 8, 8, lanes), axis=0
            )
        sums = [jnp.sum(part, axis=0, keepdims=True) for part in rows_grad]
        sums.append(jnp.zeros((8 - taps - 1, lanes), f32))
        taps_grad_ref[:, column] = jnp.concatenate(sums, axis=0)


def finish_kernel(
    x_ref, slope_ref, shared_act_ref, raw_ref, step_ref, decay_ref, d_x_ref, d_shared_ref,
    d_decay_ref, d_ssm_ref, state_in_ref, later_ref, inner_ref, rim_inner_ref,
    taps_ref, step_bias_ref, rate_ref, skip_ref, spread_ref, gather_ref,
    body_ref, edge_ref, tail_ref, taps_grad_ref, d_raw_ref, heads_ref, d_shared_out_ref,
    grad_buf, inner_buf,
    *, taps, states,
):
    length, width = x_ref.shape
    spread, gather = spread_ref[...], gather_ref[...]
    before = triangle_of("before")
    later = later_ref[...]
    grad_buf[0:rim, :] = jnp.zeros((rim, width), f32)
    grad_buf[rim + length :, :] = jnp.zeros((rim, width), f32)
    inner_buf[0:rim, :] = rim_inner_ref[...]
    inner_buf[rim:, :] = inner_ref[...]
    last = decay_ref[length - 1 : length, :]
    final = nn(two_parts(jnp.broadcast_to(jnp.exp(last), (8, lanes))), spread)[0:1, :]
    across = final * jnp.sum(
        later.astype(f32) * state_in_ref[...].astype(f32), axis=0, keepdims=True
    )
    running = nn(jnp.broadcast_to(across, (8, width)).astype(bf16), gather)[0:1, :]
    skip = skip_ref[...]
    skip_grad = jnp.zeros((1, width), f32)
    rate_grad = jnp.zeros((1, lanes), f32)
    bias_grad = jnp.zeros((1, lanes), f32)
    for rows in spans(length, chunk):
        b = shared_act_ref[rows, 0:states]
        x = x_ref[rows, :]
        step = step_ref[rows, :]
        d_ssm = d_ssm_ref[rows, :]
        fading = nn(two_parts(jnp.exp(last - decay_ref[rows, :])), spread)
        steps = nn(two_parts(step), spread)
        carrying = fading * nn(b, later)
        x_stepped = x * steps
        keys = nn((x_stepped * carrying).astype(bf16), gather)
        d_x = d_x_ref[rows, :] + carrying
        direct = nn((x * d_x).astype(bf16), gather)
        d_decay = d_decay_ref[rows, :] + running + summed_by(before, keys)
        running = running + jnp.sum(keys, axis=0, keepdims=True)
        d_shared_out_ref[rows, 0:states] = (
            d_shared_ref[rows, 0:states] + nt((x_stepped * fading).astype(bf16), later)
        )
        d_shared_out_ref[rows, states:] = d_shared_ref[rows, states:]
        skip_grad = skip_grad + jnp.sum(d_ssm * x, axis=0, keepdims=True)
        rate_grad = rate_grad + jnp.sum(step * d_decay, axis=0, keepdims=True)
        d_raw = (direct + rate_ref[...] * d_decay) * sigmoid(
            raw_ref[rows, :] + step_bias_ref[...]
        )
        d_raw_ref[rows, :] = d_raw.astype(bf16)
        bias_grad = bias_grad + jnp.sum(d_raw, axis=0, keepdims=True)
        grad_buf[pl.ds(rim + rows.start, chunk), :] = (
            skip * d_ssm + steps * d_x
        ) * slope_ref[rows, :].astype(f32)
    parts = two_parts(jnp.broadcast_to(skip_grad, (8, width)))
    skip_heads = nn(parts[:, :width], gather) + nn(parts[:, width:], gather)
    heads_ref[...] = jnp.concatenate(
        [bias_grad, rate_grad * rate_ref[...], skip_heads[0:1, :], jnp.zeros((5, lanes), f32)],
        axis=0,
    )
    filter_adjoint(
        grad_buf, inner_buf, taps_ref, length, width, taps, body_ref, edge_ref, tail_ref,
        taps_grad_ref,
    )


def shared_kernel(
    d_act_ref, slope_ref, shared_ref, rim_ref, taps_ref,
    body_ref, edge_ref, tail_ref, taps_grad_ref,
    grad_buf, inner_buf,
    *, taps,
):
    length, width = d_act_ref.shape
    grad_buf[0:rim, :] = jnp.zeros((rim, width), f32)
    grad_buf[rim + length :, :] = jnp.zeros((rim, width), f32)
    inner_buf[0:rim, :] = rim_ref[...]
    inner_buf[rim:, :] = shared_ref[...]
    grad_buf[rim : rim + length, :] = d_act_ref[...] * slope_ref[...]
    filter_adjoint(
        grad_buf, inner_buf, taps_ref, length, width, taps, body_ref, edge_ref, tail_ref,
        taps_grad_ref,
    )


def chain_kernel(pieces_ref, totals_ref, spread_ref, out_ref, *, backward):
    count = pieces_ref.shape[0]
    decays = nn(two_parts(jnp.exp(totals_ref[...])), spread_ref[...])
    state = jnp.zeros(pieces_ref.shape[1:], f32)
    order = reversed(range(count)) if backward else range(count)
    for block in order:
        out_ref[block, :, :] = state.astype(bf16)
        state = decays[block : block + 1, :] * state + pieces_ref[block].astype(f32)


def after(ready, *values):
    if not ready:
        return values if len(values) > 1 else values[0]
    tied = lax.optimization_barrier((tuple(ready), tuple(values)))[1]
    return tied if len(values) > 1 else tied[0]


def landed(ready, *transfers):
    flat = [value for transfer in transfers for value in transfer]
    flat = list(lax.optimization_barrier((tuple(ready), tuple(flat)))[1])
    return [[flat.pop(0) for _ in transfer] for transfer in transfers]


def bits_of(axis):
    return [1 << bit for bit in range(lax.axis_size(axis).bit_length() - 1)]


def swapped(value, axis, bit):
    size = lax.axis_size(axis)
    return lax.ppermute(value, axis, [(i, i ^ bit) for i in range(size)])


def passed_along(value, axis, by):
    size = lax.axis_size(axis)
    pairs = [(i, i + by) for i in range(size) if 0 <= i + by < size]
    return lax.ppermute(value, axis, pairs)


def block_at(value, index, size, dim):
    return lax.dynamic_slice_in_dim(value, index * size, size, dim)


def reversed_order(axis):
    order = [0]
    for bit in reversed(bits_of(axis)):
        order = order + [at + bit for at in order]
    return order


def relative_blocks(value, axis, dim):
    count, mine = lax.axis_size(axis), lax.axis_index(axis)
    size = value.shape[dim] // count
    blocks = [block_at(value, mine ^ other, size, dim) for other in reversed_order(axis)]
    half = len(blocks) // 2
    return [
        jnp.concatenate(blocks[:half], axis=dim),
        jnp.concatenate(blocks[half:], axis=dim),
    ]


def gathered_relative(value, axis, dim, ready=()):
    for bit in reversed(bits_of(axis)):
        value = jnp.concatenate([value, after(ready, swapped(value, axis, bit))], axis=dim)
    return value


def halves_added(kept, got, dim):
    half = got.shape[dim] // 2
    parts = [
        lax.slice_in_dim(value, at * half, (at + 1) * half, axis=dim)
        for at in range(2)
        for value in (kept, got)
    ]
    return parts[0].astype(f32) + parts[1].astype(f32), parts[2].astype(f32) + parts[3].astype(f32)


def in_place_order(value, axis, dim):
    count, mine = lax.axis_size(axis), lax.axis_index(axis)
    size = value.shape[dim] // count
    bits = bits_of(axis)

    def place(at):
        return sum(((at // bit) % 2) * back for bit, back in zip(bits, reversed(bits)))

    return jnp.concatenate(
        [block_at(value, place(mine ^ other), size, dim) for other in range(count)], axis=dim
    )


def rank_in(axis, group):
    mine = lax.axis_index(axis)
    return sum(((mine // bit) % 2) << at for at, bit in enumerate(group))


def mask_of(group, distance):
    return sum(bit for at, bit in enumerate(group) if distance >> at & 1)


class Reduction:
    def __init__(self, value, axis, groups, wire=bf16, halves=None):
        self.axis, self.wire, self.value = axis, wire, value
        self.left, self.taken = list(groups), []
        if halves is None:
            self.split()
        else:
            self.kept, self.sent = halves[0], [halves[1]]

    def split(self):
        if self.left:
            count = 1 << len(self.left[0])
            rank = rank_in(self.axis, self.left[0])
            size = self.value.shape[0] // count
            self.kept = block_at(self.value, rank, size, 0)
            self.sent = [
                block_at(self.value, rank ^ other, size, 0).astype(self.wire)
                for other in range(1, count)
            ]
        else:
            self.value = self.value.astype(bf16)
            self.sent = [self.value]

    def start(self):
        group = self.left[0] if self.left else self.taken[-1]
        count = 1 << len(group)
        sent = self.sent if self.left else self.sent * (count - 1)
        return [
            swapped(value, self.axis, mask_of(group, other))
            for other, value in enumerate(sent, 1)
        ]

    def take(self, got):
        if self.left:
            self.taken.append(self.left.pop(0))
            total = self.kept.astype(f32)
            for value in got:
                total = total + value.astype(f32)
            self.value = total.astype(self.wire)
        else:
            group = self.taken.pop()
            count = 1 << len(group)
            rank = rank_in(self.axis, group)
            if count == 2:
                low = rank == 0
                self.value = jnp.concatenate(
                    [jnp.where(low, self.value, got[0]), jnp.where(low, got[0], self.value)]
                )
            else:
                size = self.value.shape[0]
                whole = jnp.zeros((count * size,) + self.value.shape[1:], bf16)
                for other, value in enumerate([self.value] + got):
                    whole = lax.dynamic_update_slice_in_dim(
                        whole, value, (rank ^ other) * size, 0
                    )
                self.value = whole
        if self.left or self.taken:
            self.split()
        else:
            self.sent = [self.value]
        return self.sent


def exchanged_sum(value, axis):
    for bit in bits_of(axis):
        value = (value.astype(f32) + swapped(value, axis, bit).astype(f32)).astype(value.dtype)
    return value


def exchanged_all(value, axis):
    mine = lax.axis_index(axis)
    value = value[None]
    for bit in bits_of(axis):
        got = swapped(value, axis, bit)
        low = (mine // bit) % 2 == 0
        value = jnp.concatenate([jnp.where(low, value, got), jnp.where(low, got, value)], axis=0)
    return value


def to_owners(state):
    count, width = lax.axis_size("seq"), state.shape[-1]
    return [lax.all_to_all(state.reshape(count, -1, width), "seq", 0, 0, tiled=True)]


def chained(pieces, totals, states, spread, backward):
    count, size, width = pieces.shape
    mine = lax.axis_index("seq")
    here = lax.dynamic_index_in_dim(totals, mine * size // states, 1, keepdims=False)
    params, cost = cheap(10**5)
    return pl.pallas_call(
        functools.partial(chain_kernel, backward=backward),
        out_shape=jax.ShapeDtypeStruct((count, size, width), bf16),
        compiler_params=pltpu.CompilerParams(vmem_limit_bytes=vmem_limit),
        cost_estimate=cost,
    )(pieces, here, spread)


def to_blocks(scanned):
    return [lax.all_to_all(scanned, "seq", 0, 0, tiled=True)]


def on_device(
    hidden_in, norm_gain, proj_gate, proj_inner, proj_step, proj_shared, filter_inner,
    filter_inner_bias, filter_shared, filter_shared_bias, step_bias, log_rate, skip_gain,
    gate_gain, proj_out, cotangent,
):
    seqs, length, width_d = hidden_in.shape
    width = proj_gate.shape[1]
    heads = proj_step.shape[1]
    per_head = width // heads
    states = proj_shared.shape[1] // 2
    taps = filter_inner.shape[0]
    count_h = lax.axis_size("head")
    mine_h = lax.axis_index("head")
    full = width * count_h
    columns = width_d // count_h
    tokens = seqs * length
    per_device_seqs = seqs // count_h

    spread_np = np.zeros((2 * lanes, width), np.float32)
    for head in range(heads):
        spread_np[head, head * per_head : (head + 1) * per_head] = 1
        spread_np[lanes + head, head * per_head : (head + 1) * per_head] = 1
    spread = jnp.asarray(spread_np, bf16)
    gather = jnp.asarray(spread_np[:lanes].T, bf16)

    def on_lanes(vector):
        return jnp.pad(vector.astype(f32), (0, lanes - heads)).reshape(1, lanes)

    rate = on_lanes(-jnp.exp(log_rate))
    bias_row = on_lanes(step_bias)
    skip_row = jnp.repeat(skip_gain, per_head).reshape(1, width)
    gain_row = gate_gain.reshape(1, width)

    shape = jax.ShapeDtypeStruct
    wide = per_seq(length, width)
    narrow = per_seq(length, 2 * states)
    slim = per_seq(length, lanes)
    slim_t = per_seq(16, length)
    state_spec = per_seq(states, width)
    chunks = length // chunk

    normed, inner_pre, shared_pre, step_raw, inv_rms, end_inner, end_shared = grid_call(
        project_kernel,
        seqs,
        [
            per_seq(length, width_d), whole((1, width_d)), whole((width_d, width)),
            whole((width_d, 2 * states)), whole((heads, width_d)),
        ],
        [
            per_seq(length, width_d), wide, narrow, slim, slim, per_seq(rim, width),
            per_seq(rim, 2 * states),
        ],
        [
            shape((seqs, length, width_d), bf16),
            shape((seqs, length, width), f32),
            shape((seqs, length, 2 * states), f32),
            shape((seqs, length, lanes), f32),
            shape((seqs, length, lanes), f32),
            shape((seqs, rim, width), f32),
            shape((seqs, rim, 2 * states), f32),
        ],
        [],
        10**5,
    )(
        hidden_in, norm_gain.reshape(1, width_d), proj_inner, proj_shared, proj_step.T,
    )
    normed = normed.reshape(tokens, width_d)
    rim_inner = passed_along(end_inner, "seq", 1)
    rim_shared = passed_along(end_shared, "seq", 1)

    x, slope, shared_act, slope_s, step, decay, decay_t, local, total, state = grid_call(
        functools.partial(states_kernel, taps=taps, states=states),
        seqs,
        [
            wide, per_seq(rim, width), narrow, per_seq(rim, 2 * states), slim,
            whole((taps, width)), whole((1, width)), whole((taps, 2 * states)),
            whole((1, 2 * states)), whole((1, lanes)), whole((1, lanes)), whole((2 * lanes, width)),
        ],
        [
            wide, wide, narrow, narrow, slim, slim, slim_t, per_seq(chunks, states, width),
            per_seq(8, lanes), state_spec,
        ],
        [
            shape((seqs, length, width), f32),
            shape((seqs, length, width), bf16),
            shape((seqs, length, 2 * states), bf16),
            shape((seqs, length, 2 * states), f32),
            shape((seqs, length, lanes), f32),
            shape((seqs, length, lanes), f32),
            shape((seqs, 16, length), f32),
            shape((seqs, chunks, states, width), bf16),
            shape((seqs, 8, lanes), f32),
            shape((seqs, states, width), bf16),
        ],
        [
            pltpu.VMEM((rim + length, width), f32),
            pltpu.VMEM((rim + length, 2 * states), f32),
            pltpu.VMEM((chunk, width), bf16),
        ],
        10**5,
    )(
        inner_pre, rim_inner, shared_pre, rim_shared, step_raw, filter_inner,
        filter_inner_bias.reshape(1, width), filter_shared,
        filter_shared_bias.reshape(1, 2 * states), bias_row, rate, spread,
    )
    local_out = grid_call(
        functools.partial(mix_kernel, states=states),
        seqs,
        [
            wide, narrow, slim, slim, slim_t, per_seq(chunks, states, width), whole((1, width)),
            whole((2 * lanes, width)),
        ],
        wide,
        shape((seqs, length, width), f32),
        [],
        10**5,
    )(x, shared_act, step, decay, decay_t, local, skip_row, spread)

    cot_near = after([state], cotangent.reshape(tokens, columns))
    totals = exchanged_all(after([local_out], total[:, 0, :]), "seq")
    (pieces,), (cot_far,) = landed(
        [totals], to_owners(state), [swapped(cot_near, "head", bits_of("head")[-1])]
    )
    scanned = chained(pieces, totals, states, spread, False)
    cot_all = jnp.concatenate([cot_near, cot_far], axis=1)
    for bit in reversed(bits_of("head")[:-1]):
        cot_all = jnp.concatenate([cot_all, swapped(cot_all, "head", bit)], axis=1)
    gate_pre = nn(after([scanned], normed), proj_gate).reshape(seqs, length, width)
    out_kept, out_sent = relative_blocks(after([scanned], proj_out), "head", 1)
    out_kept, out_sent = after([gate_pre], out_kept, out_sent)
    middle = cot_all.shape[1] // 2
    mixer_grad = nt(cot_all[:, :middle], out_kept) + nt(cot_all[:, middle:], out_sent)
    mixer_grad = mixer_grad.reshape(seqs, length, width)
    ((state_in,),) = landed([gate_pre, mixer_grad], to_blocks(scanned))
    cot_all = after([gate_pre], cot_all)
    state_in = state_in.reshape(seqs, states, width)

    ssm_out, sums = grid_call(
        functools.partial(gate_kernel, states=states),
        seqs,
        [
            wide, narrow, slim, state_spec, wide, wide, whole((1, width)),
            whole((2 * lanes, width)),
        ],
        [wide, per_seq(8, length)],
        [shape((seqs, length, width), f32), shape((seqs, 8, length), f32)],
        [pltpu.VMEM((length, width), bf16), pltpu.VMEM((length, width), bf16)],
        10**5,
    )(local_out, shared_act, decay, state_in, gate_pre, mixer_grad, gain_row, spread)
    sums_all = lax.all_gather(sums, "head")

    mixer_in, d_gate, d_ssm, lam, gain_grad = grid_call(
        functools.partial(gate_back_kernel, states=states, full=float(full)),
        seqs,
        [
            wide, wide, wide,
            pl.BlockSpec((count_h, None, 8, length), lambda s: (0, s, 0, 0)),
            whole((1, width)), narrow, slim, whole((2 * lanes, width)),
        ],
        [wide, wide, wide, state_spec, per_seq(8, width)],
        [
            shape((seqs, length, width), bf16),
            shape((seqs, length, width), bf16),
            shape((seqs, length, width), f32),
            shape((seqs, states, width), bf16),
            shape((seqs, 8, width), f32),
        ],
        [],
        10**5,
    )(ssm_out, gate_pre, mixer_grad, sums_all, gain_row, shared_act, decay, spread)

    mixer_flat = mixer_in.reshape(tokens, width)
    d_gate_flat = d_gate.reshape(tokens, width)
    bits = bits_of("seq")
    groups = [bits[:1], bits[1:]]

    def in_parts(left, right, first, rows, ready):
        half, upper = rows // 2, rank_in("seq", bits[:1])
        far = product(tn, after(ready, left), right, bf16, first + (1 - upper) * half, half)
        near = product(tn, after([far], left), right, bf16, first + upper * half, half)
        return near, far

    near_bit, far_bit = bits_of("head")
    out_parts = in_parts(mixer_flat, cot_all, 0, width, ())
    out_sum = Reduction(None, "seq", groups, halves=out_parts)
    gate_parts = in_parts(normed, d_gate_flat, 0, width_d, out_parts[:1])
    gate_sum = Reduction(None, "seq", groups, halves=gate_parts)

    def mix_back(first, count, d_ssm, into):
        def at(*dims):
            return per_seq(*dims, first=first)

        wide, narrow, slim = at(length, width), at(length, 2 * states), at(length, lanes)
        return grid_call(
            functools.partial(mix_back_kernel, states=states),
            count,
            [
                wide, narrow, slim, slim, at(16, length), at(chunks, states, width),
                at(states, width), wide, whole((2 * lanes, width)), whole((width, lanes)),
            ],
            [wide, narrow, slim],
            [
                shape((seqs, length, width), f32),
                shape((seqs, length, 2 * states), f32),
                shape((seqs, length, lanes), f32),
            ],
            [pltpu.VMEM((lanes, chunk), f32)],
            10**5,
            into,
        )(x, shared_act, step, decay, decay_t, local, state_in, d_ssm, spread, gather)

    quarter = seqs // 4
    back_parts = mix_back(0, quarter, after(gate_parts[:1], d_ssm), ())
    (pieces,), got = landed([back_parts[2]], to_owners(lam), out_sum.start())
    scanned = chained(pieces, totals, states, spread, True)
    ready = [scanned] + out_sum.take(got) + gate_sum.sent
    back_parts = mix_back(quarter, seqs - quarter, after(ready, d_ssm), back_parts)
    d_x, d_shared, d_decay = back_parts
    sent_out = product(nn, after([d_decay], mixer_flat), out_sent, bf16)
    kept_out = product(nn, after([sent_out], mixer_flat), out_kept, bf16)
    (later,), got, got_gate = landed(
        [kept_out], to_blocks(scanned), out_sum.start(), gate_sum.start()
    )
    later = later.reshape(seqs, states, width)
    out_sum.take(got)
    ready = gate_sum.take(got_gate)
    sent_out = after(ready, sent_out)

    def finish(first, count, later, into):
        def at(*dims):
            return per_seq(*dims, first=first)

        wide, narrow, slim = at(length, width), at(length, 2 * states), at(length, lanes)
        state_spec = at(states, width)
        return grid_call(
            functools.partial(finish_kernel, taps=taps, states=states),
            count,
            [
                wide, wide, narrow, slim, slim, slim, wide, narrow, slim, wide, state_spec, state_spec,
                wide, at(rim, width), whole((taps, width)), whole((1, lanes)), whole((1, lanes)),
                whole((1, width)), whole((2 * lanes, width)), whole((width, lanes)),
            ],
            [
                wide, at(rim, width), at(rim, width), at(8, width), slim,
                at(8, lanes), narrow,
            ],
            [
                shape((seqs, length, width), bf16),
                shape((seqs, rim, width), bf16),
                shape((seqs, rim, width), f32),
                shape((seqs, 8, width), f32),
                shape((seqs, length, lanes), bf16),
                shape((seqs, 8, lanes), f32),
                shape((seqs, length, 2 * states), f32),
            ],
            [
                pltpu.VMEM((2 * rim + length, width), f32),
                pltpu.VMEM((rim + length, width), f32),
            ],
            10**5,
            into,
        )(
            x, slope, shared_act, step_raw, step, decay, d_x, d_shared, d_decay, d_ssm, state_in,
            later, inner_pre, rim_inner, filter_inner, bias_row, rate, skip_row, spread, gather,
        )


    body, edge, tail, taps_grad, d_raw, heads_grad, d_act = finish(
        0, seqs, after(ready, later), ()
    )

    def joined(body, edge, tail):
        ends = (tail + passed_along(edge, "seq", -1).astype(f32)).astype(bf16)
        return lax.dynamic_update_slice_in_dim(body, ends, length - rim, 1)

    d_act_kept, d_act_sent = relative_blocks(d_act, "head", 0)
    got, (got_out,) = landed(
        [body], gate_sum.start(), [swapped(sent_out, "head", near_bit)]
    )
    mixed, sent_out = halves_added(kept_out, got_out, 1)
    sent_out = sent_out.astype(bf16)
    ready = gate_sum.take(got) + [sent_out]
    step_grad = product(tn, after(ready, d_raw.reshape(tokens, lanes)), normed, f32)
    (edge,), (got_act,) = landed(
        [step_grad], [passed_along(edge, "seq", -1)], [swapped(d_act_sent, "head", near_bit)]
    )
    d_act_kept, d_act_sent = halves_added(d_act_kept, got_act, 0)

    def joined(body, edge, tail):
        ends = (tail + edge.astype(f32)).astype(bf16)
        return lax.dynamic_update_slice_in_dim(body, ends, length - rim, 1)

    d_inner = joined(body, edge, tail)
    d_inner_flat = d_inner.reshape(tokens, width)
    inner_parts = in_parts(normed, d_inner_flat, 0, width_d, [d_inner, d_act_sent])
    inner_sum = Reduction(None, "seq", groups, halves=inner_parts)
    (got_act,), got, (got_out,) = landed(
        inner_parts[:1], [swapped(d_act_sent, "head", far_bit)], out_sum.start(),
        [swapped(sent_out, "head", far_bit)],
    )
    ready = out_sum.take(got)
    mixed = (mixed + got_out.astype(f32)).reshape(seqs, length, columns)
    blocks = [mine_h ^ other for other in reversed_order("head")]
    middle = len(blocks) // 2
    step_rows = jnp.pad(after([d_inner], proj_step).T, ((0, 16 - heads), (0, 0)))
    ready, back = ready + [step_rows], []
    for picked in (blocks[middle:], blocks[:middle]):
        back.append(
            back_product(
                jnp.stack(picked), columns, d_gate, after(ready, d_inner), d_raw, proj_gate,
                proj_inner, step_rows, bf16,
            )
        )
        ready = back[-1:]
    got, got_gate = landed(ready, inner_sum.start(), gate_sum.start())
    ready = inner_sum.take(got) + gate_sum.take(got_gate)
    back = list(after(ready, *back))

    d_act_own = d_act_kept + got_act
    own = [
        block_at(value, mine_h, per_device_seqs, 0)
        for value in after(ready, slope_s, shared_pre, rim_shared)
    ]
    s_body, s_edge, s_tail, s_taps_grad = grid_call(
        functools.partial(shared_kernel, taps=taps),
        per_device_seqs,
        [narrow, narrow, narrow, per_seq(rim, 2 * states), whole((taps, 2 * states))],
        [narrow, per_seq(rim, 2 * states), per_seq(rim, 2 * states), per_seq(8, 2 * states)],
        [
            shape((per_device_seqs, length, 2 * states), bf16),
            shape((per_device_seqs, rim, 2 * states), bf16),
            shape((per_device_seqs, rim, 2 * states), f32),
            shape((per_device_seqs, 8, 2 * states), f32),
        ],
        [
            pltpu.VMEM((2 * rim + length, 2 * states), f32),
            pltpu.VMEM((rim + length, 2 * states), f32),
        ],
        10**5,
    )(after(ready, d_act_own), own[0], own[1], own[2], filter_shared)
    (s_edge,), (got_back,) = landed(
        [s_body], [passed_along(s_edge, "seq", -1)], [swapped(back[0], "head", near_bit)]
    )
    d_normed, back_sent = halves_added(back[1], got_back, 1)
    back_sent = back_sent.astype(bf16)
    s_edge = after([back_sent], s_edge)
    taps_rows = jnp.zeros((per_device_seqs, rim, 2 * states), bf16)
    taps_rows = lax.dynamic_update_slice(taps_rows, s_taps_grad.astype(bf16), (0, 0, 0))
    d_shared_all = jnp.concatenate([joined(s_body, s_edge, s_tail), taps_rows], axis=1)
    d_shared_all = gathered_relative(d_shared_all, "head", 0)
    d_shared_all = in_place_order(d_shared_all, "head", 0)
    s_taps_sum = jnp.sum(d_shared_all[:, length:].astype(f32), axis=0)
    d_shared_flat = d_shared_all[:, :length].reshape(tokens, 2 * states)
    shared_rows = product(tn, normed, d_shared_flat, f32, mine_h * columns, columns)
    shared_rows = jnp.concatenate([shared_rows, s_taps_sum[:8], jnp.zeros((16, 2 * states), f32)])

    got, got_out, (got_back,) = landed(
        [shared_rows], inner_sum.start(), out_sum.start(),
        [swapped(back_sent, "head", far_bit)],
    )
    ready = inner_sum.take(got)
    out_sum.take(got_out)
    d_normed = after(ready, d_normed) + got_back.astype(f32)
    d_normed = d_normed + nt(d_shared_flat, block_at(proj_shared, mine_h, columns, 0))
    d_normed = d_normed.reshape(seqs, length, columns)
    ready = ready + [shared_rows]
    hidden_own = block_at(after(ready, hidden_in), mine_h, columns, 2).astype(f32)
    activations = (hidden_own + mixed).astype(bf16)
    scaled = d_normed * block_at(after(ready, norm_gain), mine_h, columns, 0)
    norm_row = jnp.sum(scaled * hidden_own, axis=-1)
    inv_rms = after(ready, inv_rms)[:, :, :1]
    norm_row = jnp.sum(lax.all_gather(norm_row, "head"), axis=0)[..., None] / width_d
    grad_input = (
        cotangent.astype(f32)
        + inv_rms * scaled
        - hidden_own * inv_rms * inv_rms * inv_rms * norm_row
    )
    norm_gain_grad = jnp.sum(d_normed * hidden_own * inv_rms, axis=(0, 1))

    step_grad, taps_grad, gain_grad, heads_grad = after(
        ready, step_grad, taps_grad, gain_grad, heads_grad
    )
    step_grad = step_grad[:16].reshape(32, width_d // 2)
    rows_small = jnp.concatenate(
        [
            jnp.sum(taps_grad, axis=0),
            jnp.sum(gain_grad, axis=0)[:1],
            jnp.pad(jnp.sum(heads_grad, axis=0)[:3], ((0, 0), (0, width - lanes))),
            jnp.zeros((4, width), f32),
        ],
        axis=0,
    )
    part = shared_rows.shape[0] * 2 * states // width
    shared_wide = jnp.concatenate(
        [shared_rows[at * part : (at + 1) * part] for at in range(width // (2 * states))], axis=1
    )
    small = jnp.concatenate([rows_small, step_grad, shared_wide], axis=0)
    count = lax.axis_size("seq")
    small = jnp.pad(small, ((0, -small.shape[0] % (8 * count)), (0, 0)))
    small = lax.all_to_all(small.reshape(count, -1, width), "seq", 0, 0, tiled=True)
    small = jnp.broadcast_to(jnp.sum(small, axis=0, keepdims=True).astype(bf16), small.shape)
    small = lax.all_to_all(small, "seq", 0, 0, tiled=True).astype(f32).reshape(-1, width)
    norm_gain_grad = exchanged_sum(norm_gain_grad, "seq")
    step_out = small[16:48].reshape(16, width_d)[:heads].T
    shared_back = jnp.concatenate(
        [
            small[48 : 48 + part, at * 2 * states : (at + 1) * 2 * states]
            for at in range(width // (2 * states))
        ],
        axis=0,
    ).astype(bf16)
    shared_full = in_place_order(gathered_relative(shared_back[None], "head", 0), "head", 0)
    shared_full = shared_full.astype(f32)
    shared_out = shared_full[:, :columns].reshape(width_d, 2 * states)
    shared_extra = shared_full[0, columns : columns + 8]

    out_grad = in_place_order(out_sum.value, "head", 1).astype(f32)
    got, got_gate = landed([grad_input, norm_gain_grad], inner_sum.start(), gate_sum.start())
    ready = inner_sum.take(got)
    gate_out = gate_sum.take(got_gate)[0].astype(f32)
    out_grad, gate_out, small = after(ready, out_grad, gate_out, small)
    ((*got,),) = landed([out_grad, gate_out, small], inner_sum.start())
    inner_out = inner_sum.take(got)[0].astype(f32)
    return (
        activations,
        grad_input,
        norm_gain_grad,
        gate_out,
        inner_out,
        step_out,
        shared_out,
        small[:taps],
        small[taps],
        shared_extra[:taps],
        shared_extra[taps],
        small[9, :heads],
        small[10, :heads],
        small[11, :heads],
        small[8],
        out_grad,
    )


def solution(mesh):
    in_specs = (
        P(None, "seq", None),
        P(),
        P(None, "head"),
        P(None, "head"),
        P(None, "head"),
        P(),
        P(None, "head"),
        P("head"),
        P(),
        P(),
        P("head"),
        P("head"),
        P("head"),
        P("head"),
        P("head", None),
        P(None, "seq", "head"),
    )
    out_specs = (
        P(None, "seq", "head"),
        P(None, "seq", "head"),
        P("head"),
        P(None, "head"),
        P(None, "head"),
        P(None, "head"),
        P(),
        P(None, "head"),
        P("head"),
        P(),
        P(),
        P("head"),
        P("head"),
        P("head"),
        P("head"),
        P("head", None),
    )
    return jax.shard_map(
        on_device, mesh=mesh, in_specs=in_specs, out_specs=out_specs, check_vma=False
    )
```

time: 1520 us -> 524 us (0.34)
  waiting for transfers between devices: 864 us -> 77.7 us
  matrix products: 277 us -> 20 us
  Pallas kernels: 0 us -> 184 us
  other arithmetic: 192 us -> 61.1 us
  starting transfers between devices: 13 us -> 107 us
  blocking collectives: 78.7 us -> 12.8 us
  local copies, waits for them, and re-layouts: 79.1 us -> 51.6 us
    psum x2 -> x0, waiting for transfers between devices: 596 us -> none  [the longest x1 435 us: on_device(): lax.psum((grad_norm_gain, grad_proj_gate, grad_proj_inner, grad_proj_step...]
    dot_general x27 -> x4, matrix products: 277 us -> 20 us  [the longest x3 11.6 us: nt(): lax.dot_general(left, right, (((1,), (1,)), ((), ())), preferred_element_...]
    all_gather x3 -> x0, waiting for transfers between devices: 210 us -> none  [the longest x2 210 us: prefix(): pieces = jax.tree.map(lambda part: lax.all_gather(part, axis), value)]
    pallas_call x0 -> x23, Pallas kernels: none -> 184 us  [the longest x9 111 us: grid_call(): return lambda *operands: call(*operands, *into)]
    ppermute x4 -> x46, waiting for transfers between devices: 0.01 us -> 60.4 us  [the longest x42 55.4 us: swapped(): return lax.ppermute(value, axis, [(i, i ^ bit) for i in range(size)])]
    ppermute x4 -> x46, starting transfers between devices: 12.5 us -> 72.5 us  [the longest x42 61.6 us: swapped(): return lax.ppermute(value, axis, [(i, i ^ bit) for i in range(size)])]
    reduce_scatter x1 -> x0, waiting for transfers between devices: 56.9 us -> none  [on_device(): lax.psum_scatter(partial_out, 'head', scatter_dimension=2, tiled=True)]
    psum x3 -> x0, blocking collectives: 52.1 us -> none  [the longest x1 39.7 us: on_device(): lax.psum((grad_norm_gain, grad_proj_gate, grad_proj_inner, grad_proj_step...]
  transfers between devices with their start and end apart: 10 -> 52, of which waited for: 5 -> 15; matrix products, arithmetic and copies ran while one was open for 20% -> 20% of each run, Pallas kernels for 0% -> 26%
where the time goes in v1:
time: 524 us; the launch traced here: 516 us
  Pallas kernels  184 us (35%)
  starting transfers between devices  107 us (20%)
  waiting for transfers between devices  77.7 us (15%)
  other arithmetic  61.1 us (12%)
  local copies, waits for them, and re-layouts  51.6 us (10%)
  matrix products  20 us (4%)
  blocking collectives  12.8 us (2%)
    pallas_call x9, Pallas kernels, grid_call(): return lambda *operands: call(*operands, *into)  111 us
    ppermute x42, starting transfers between devices, swapped(): return lax.ppermute(value, axis, [(i, i ^ bit) for i in range(size)])  61.6 us
    ppermute x42, waiting for transfers between devices, swapped(): return lax.ppermute(value, axis, [(i, i ^ bit) for i in range(size)])  55.4 us
    pallas_call x10, Pallas kernels, product(): pl.pallas_call(functools.partial(product_kernel, dot=dot), grid_spec=pltp...  49.1 us
    pallas_call x2, Pallas kernels, back_product(): pl.pallas_call(functools.partial(back_kernel, parts=parts), grid_spec=plt...  18.6 us
    all_to_all x1, waiting for transfers between devices, on_device(): lax.all_to_all(small, 'seq', 0, 0, tiled=True).astype(f32)  17.3 us
    dynamic_update_slice x9, local copies, waits for them, and re-layouts, take(): lax.dynamic_update_slice_in_dim(whole, value, (rank ^ other) * size, 0)  13.3 us
    all_to_all x2, starting transfers between devices, to_owners(): lax.all_to_all(state.reshape(count, -1, width), 'seq', 0, 0, tiled=True)  13.3 us
  transfers between devices with their start and end apart: 52, of which 15 were waited for; matrix products, arithmetic and copies ran while one was open for 20% of the time, Pallas kernels for 26%

profile of v1, /device:TPU:0, one launch (start us, length us, event | category | flops | bytes accessed | tf_op | source)
XLA Modules:
  0.0 515.8 jit_solution(7187669122458696270)
XLA Ops:
  1.9 11.1 %shard_map.297 = (bf16[4,384,1536]{2,1,0:T(8,128)(2,1)}, f32[4,384,768]{2,1,0:T(8,128)}, f32[4,384,256]{2,1,0:T(8,128)}, f32[4,384,128]{2,1,0:T(8,128)}, f32[4,3...) custom-call(bf16[4,384,1536]{2,1,0:T(8,128)(2,1)} %refs_0_.3, f32[1,1536]{1,0:T(1,128)} %reshape.188.refs_1_, ...), custom_call_target="tpu_custom_call" | custom-call | flops 100000 | bytes 100000 | tf_op jit(solution)/shard_map/pallas_call | solution.py:95
  24.5 15.0 %shard_map.298 = (f32[4,384,768]{2,1,0:T(8,128)}, bf16[4,384,768]{2,1,0:T(8,128)(2,1)}, bf16[4,384,256]{2,1,0:T(8,128)(2,1)}, f32[4,384,256]{2,1,0:T(8,128)}, f3...) custom-call(f32[4,384,768]{2,1,0:T(8,128)} %get-tuple-element.134.re, ...), custom_call_target="tpu_custom_call" | custom-call | flops 100000 | bytes 100000 | tf_op jit(solution)/shard_map/pallas_call | solution.py:95
  39.5 6.7 %all-to-all-start = ((bf16[8,64,768]{2,1,0:T(8,128)(2,1)}), bf16[8,64,768]{2,1,0:T(8,128)(2,1)S(1)}, u32[]{:S(2)}, u32[]{:S(2)}) async-start(bf16[8,64,768]{2,1,0:T(8,128)(2,1)} %bitcast.102), calls=%async_computation | async-start | bytes 1572864 | tf_op jit(solution)/shard_map/all_to_all | solution.py:759
  48.6 8.8 %shard_map.299.refs_0_ = f32[4,384,768]{2,1,0:T(8,128)} custom-call(f32[4,384,768]{2,1,0:T(8,128)} %get-tuple-element.139.refs_0_, bf16[4,384,256]{2,1,0:T(8,128)(2,1)} %get-tuple-element.141.refs_1_.refs_5_.refs_2_, f32[4,384,128]{2,1,0:T(8,128)} %get-tuple-element.142.refs_2_.refs_4_, f32[4,384,128]{2,1,0:T(8,128)} %get-tuple-element.143.refs_3_.refs_2_.refs_6_.refs_5_, ...), custom_call_target="tpu_custom_call" | custom-call | flops 100000 | bytes 100000 | tf_op jit(solution)/shard_map/pallas_call | solution.py:95
  61.3 11.7 %collective-permute-done.5 = bf16[1536,384]{1,0:T(8,128)(2,1)S(1)} collective-permute-done((bf16[1536,384]{1,0:T(8,128)(2,1)S(1)}, bf16[1536,384]{1,0:T(8,128)(2,1)S(1)}, u32[]{:S(2)}, u32[]{:S(2)}) %collective-permute-start.5) | collective-permute-done | bytes 1179680 | tf_op jit(solution)/shard_map/ppermute | solution.py:609
  85.7 6.0 %all-to-all-start.1 = ((bf16[8,64,768]{2,1,0:T(8,128)(2,1)}), bf16[8,64,768]{2,1,0:T(8,128)(2,1)S(1)}, u32[]{:S(2)}, u32[]{:S(2)}) async-start(bf16[8,64,768]{2,1,0:T(8,128)(2,1)} %shard_map.300), calls=%async_computation.1 | async-start | bytes 1572864 | tf_op jit(solution)/shard_map/all_to_all | solution.py:776
  94.1 8.4 %fusion.18 = f32[1536,768]{1,0:T(8,128)} fusion(bf16[1536,1536]{1,0:T(8,128)(2,1)} %bitcast.65, bf16[1536,768]{1,0:T(8,128)(2,1)S(1)} %copy-done), kind=kOutput, calls=%fused_computation.140 | convolution fusion | flops 3623878656 | bytes 11796480 | tf_op jit(solution)/shard_map/dot_general | solution.py:21
  112.3 9.1 %shard_map.301 = (f32[4,384,768]{2,1,0:T(8,128)}, f32[4,8,384]{2,1,0:T(8,128)}) custom-call(f32[4,384,768]{2,1,0:T(8,128)} %shard_map.299.refs_0_, bf16[4,384,256]{2,1,0:T(8,128)(2,1)} %get-tuple-element.141.refs_1_.refs_5_.refs_2_, f32[4,384,128]{2,1,0:T(8,128)} %get-tuple-element.143.refs_3_.refs_2_.refs_6_.refs_5_, bf16[4,128,768]{2,1,0:T(8,128)(2,1)} %bitcast.82, ...), custom_call_target="tpu_custom_call" | custom-call | flops 100000 | bytes 100000 | tf_op jit(solution)/shard_map/pallas_call | solution.py:95
  121.4 7.2 %all-gather = f32[16,8,384]{2,1,0:T(8,128)} all-gather(f32[4,8,384]{2,1,0:T(8,128)} %get-tuple-element.159), channel_id=2, replica_groups=mesh['seq'=8,'head'=4] {'head'}, dimensions={0}, use_global_device_ids=true | all-gather | bytes 245760 | tf_op jit(solution)/shard_map/all_gather | solution.py:928
  128.6 12.2 %shard_map.302 = (bf16[4,384,768]{2,1,0:T(8,128)(2,1)}, bf16[4,384,768]{2,1,0:T(8,128)(2,1)}, f32[4,384,768]{2,1,0:T(8,128)}, bf16[4,128,768]{2,1,0:T(8,128)(2,1)}, f32[4,8,768]{2,1,0:T(8,128)}) custom-call(f32[4,384,768]{2,1,0:T(8,128)} %get-tuple-element.158.refs_0_, f32[4,384,768]{2,1,0:T(8,128)} %bitcast.87, f32[4,384,768]{2,1,0:T(8,128)} %bitcast.89, ...), custom_call_target="tpu_custom_call" | custom-call | flops 100000 | bytes 100000 | tf_op jit(solution)/shard_map/pallas_call | solution.py:95
  140.8 6.6 %all-to-all-start.2 = ((bf16[8,64,768]{2,1,0:T(8,128)(2,1)}), bf16[8,64,768]{2,1,0:T(8,128)(2,1)S(1)}, u32[]{:S(2)}, u32[]{:S(2)}) async-start(bf16[8,64,768]{2,1,0:T(8,128)(2,1)} %bitcast.101), calls=%async_computation.2 | async-start | bytes 1572864 | tf_op jit(solution)/shard_map/all_to_all | solution.py:759
  151.1 5.8 %shard_map.303 = bf16[384,1536]{1,0:T(8,128)(2,1)} custom-call(s32[1]{0:T(128)} %bitcast.16.at_ref, bf16[1536,768]{1,0:T(8,128)(2,1)} %bitcast.76, bf16[1536,1536]{1,0:T(8,128)(2,1)} %pad_maximum_fusion.right_ref), custom_call_target="tpu_custom_call" | custom-call | flops 100000 | bytes 100000 | tf_op jit(solution)/shard_map/pallas_call | solution.py:118
  158.9 5.7 %shard_map.304 = bf16[384,1536]{1,0:T(8,128)(2,1)} custom-call(s32[1]{0:T(128)} %bitcast.15.at_ref, bf16[1536,768]{1,0:T(8,128)(2,1)} %bitcast.77, bf16[1536,1536]{1,0:T(8,128)(2,1)} %pad_maximum_fusion.right_ref), custom_call_target="tpu_custom_call" | custom-call | flops 100000 | bytes 100000 | tf_op jit(solution)/shard_map/pallas_call | solution.py:118
  174.9 9.4 %shard_map.307 = (f32[4,384,768]{2,1,0:T(8,128)}, f32[4,384,256]{2,1,0:T(8,128)}, f32[4,384,128]{2,1,0:T(8,128)}) custom-call(f32[4,384,768]{2,1,0:T(8,128)} %get-tuple-element.139.refs_0_, bf16[4,384,256]{2,1,0:T(8,128)(2,1)} %get-tuple-element.141.refs_1_.refs_5_.refs_2_, f32[4,384,128]{2,1,0:T(8,128)} %get-tuple-element.142.refs_2_.refs_4_, ...), custom_call_target="tpu_custom_call" | custom-call | flops 100000 | bytes 100000 | tf_op jit(solution)/shard_map/pallas_call | solution.py:95
  191.6 5.7 %all-to-all-start.3 = ((bf16[8,64,768]{2,1,0:T(8,128)(2,1)}), bf16[8,64,768]{2,1,0:T(8,128)(2,1)S(1)}, u32[]{:S(2)}, u32[]{:S(2)}) async-start(bf16[8,64,768]{2,1,0:T(8,128)(2,1)} %shard_map.308), calls=%async_computation.3 | async-start | bytes 1572864 | tf_op jit(solution)/shard_map/all_to_all | solution.py:776
  207.3 22.7 %shard_map.309 = (f32[4,384,768]{2,1,0:T(8,128)}, f32[4,384,256]{2,1,0:T(8,128)}, f32[4,384,128]{2,1,0:T(8,128)}) custom-call(f32[4,384,768]{2,1,0:T(8,128)} %get-tuple-element.139.refs_0_, bf16[4,384,256]{2,1,0:T(8,128)(2,1)} %get-tuple-element.141.refs_1_.refs_5_.refs_2_, ...), custom_call_target="tpu_custom_call", output_to_operand_aliasing={{0}: (10, {}), {1}: (11, {}), {2}: (12, {})} | custom-call | flops 100000 | bytes 100000 | tf_op jit(solution)/shard_map/pallas_call | solution.py:95
  250.3 20.0 %shard_map.312 = (bf16[4,384,768]{2,1,0:T(8,128)(2,1)}, bf16[4,16,768]{2,1,0:T(8,128)(2,1)}, f32[4,16,768]{2,1,0:T(8,128)}, f32[4,8,768]{2,1,0:T(8,128)}, bf16[4...) custom-call(f32[4,384,768]{2,1,0:T(8,128)} %get-tuple-element.139.refs_0_, ...), custom_call_target="tpu_custom_call" | custom-call | flops 100000 | bytes 100000 | tf_op jit(solution)/shard_map/pallas_call | solution.py:95
  309.0 12.0 %collective-permute-done.20 = bf16[96,1536]{1,0:T(8,128)(2,1)} collective-permute-done((bf16[96,1536]{1,0:T(8,128)(2,1)}, bf16[96,1536]{1,0:T(8,128)(2,1)}, u32[]{:S(2)}, u32[]{:S(2)}) %collective-permute-start.20) | collective-permute-done | bytes 294944 | tf_op jit(solution)/shard_map/ppermute | solution.py:609
  332.8 9.2 %shard_map.316 = bf16[1536,768]{1,0:T(8,128)(2,1)} custom-call(s32[2]{0:T(128)} %pad_add_fusion.1.blocks_ref, bf16[4,384,768]{2,1,0:T(8,128)(2,1)} %get-tuple-element.164.gate_ref, bf16[4,384,768]{2,1,0:T(8,128)(2,1)} %fusion.14.inner_ref, bf16[4,384,128]{2,1,0:T(8,128)(2,1)} %get-tuple-element.190.raw_ref, bf16[1536,768]{1,0:T(8,128)(2,1)} %refs_1_.3, ...), custom_call_target="tpu_custom_call" | custom-call | flops 100000 | bytes 100000 | tf_op jit(solution)/shard_map/pallas_call | solution.py:167
  342.0 9.4 %shard_map.317 = bf16[1536,768]{1,0:T(8,128)(2,1)} custom-call(s32[2]{0:T(128)} %pad_add_fusion.blocks_ref, bf16[4,384,768]{2,1,0:T(8,128)(2,1)} %get-tuple-element.164.gate_ref, bf16[4,384,768]{2,1,0:T(8,128)(2,1)} %fusion.14.inner_ref, bf16[4,384,128]{2,1,0:T(8,128)(2,1)} %get-tuple-element.190.raw_ref, bf16[1536,768]{1,0:T(8,128)(2,1)} %refs_1_.3, ...), custom_call_target="tpu_custom_call" | custom-call | flops 100000 | bytes 100000 | tf_op jit(solution)/shard_map/pallas_call | solution.py:167
  404.4 9.6 %collective-permute-done.34 = bf16[384,1536]{1,0:T(8,128)(2,1)} collective-permute-done((bf16[384,1536]{1,0:T(8,128)(2,1)}, bf16[384,1536]{1,0:T(8,128)(2,1)}, u32[]{:S(2)}, u32[]{:S(2)}) %collective-permute-start.34) | collective-permute-done | bytes 1179680 | tf_op jit(solution)/shard_map/ppermute | solution.py:609
  414.0 5.8 %collective-permute-done.35 = bf16[1536,384]{1,0:T(8,128)(2,1)S(1)} collective-permute-done((bf16[1536,384]{1,0:T(8,128)(2,1)S(1)}, bf16[1536,384]{1,0:T(8,128)(2,1)S(1)}, u32[]{:S(2)}, u32[]{:S(2)}) %collective-permute-start.35) | collective-permute-done | bytes 1179680 | tf_op jit(solution)/shard_map/ppermute | solution.py:609
  443.1 5.6 %all-gather.2 = f32[4,4,384]{2,1,0:T(4,128)} all-gather(f32[1,4,384]{2,1,0:T(4,128)S(1)} %bitcast.108), channel_id=3, replica_groups=mesh['seq'=8,'head'=4] {'head'}, dimensions={0}, use_global_device_ids=true | all-gather | bytes 30720 | tf_op jit(solution)/shard_map/all_gather | solution.py:1150
  484.2 17.3 %all-to-all-done.5 = bf16[8,24,768]{2,1,0:T(8,128)(2,1)S(1)} async-done(((bf16[8,24,768]{2,1,0:T(8,128)(2,1)}), bf16[8,24,768]{2,1,0:T(8,128)(2,1)S(1)}, u32[]{:S(2)}, u32[]{:S(2)}) %all-to-all-start.5) | async-done | bytes 294944 | tf_op jit(solution)/shard_map/all_to_all | solution.py:1180
  (341 shorter events, 272.9 us)
Async XLA Ops:
  39.5 33.4 %all-to-all-start = ((bf16[8,64,768]{2,1,0:T(8,128)(2,1)}), bf16[8,64,768]{2,1,0:T(8,128)(2,1)S(1)}, u32[]{:S(2)}, u32[]{:S(2)}) async-start(bf16[8,64,768]{2,1,0:T(8,128)(2,1)} %bitcast.102), calls=%async_computation | async-start | bytes 1572864 | tf_op jit(solution)/shard_map/all_to_all | solution.py:759
  74.3 28.4 %collective-permute-start.6 = (bf16[1536,768]{1,0:T(8,128)(2,1)}, bf16[1536,768]{1,0:T(8,128)(2,1)}, u32[]{:S(2)}, u32[]{:S(2)}) collective-permute-start(bf16[1536,768]{1,0:T(8,128)(2,1)} %constant_dynamic-update-slice_fusion.13), channel_id=1, source_target_pairs={{0,1},{1,0},{2,3},{3,2},{4,5},{5,4},{6,7},{7,6},{8,9},{9,8},{10,11... | collective-permute-start | bytes 7077896 | tf_op jit(solution)/shard_map/ppermute | solution.py:609
  140.8 46.3 %all-to-all-start.2 = ((bf16[8,64,768]{2,1,0:T(8,128)(2,1)}), bf16[8,64,768]{2,1,0:T(8,128)(2,1)S(1)}, u32[]{:S(2)}, u32[]{:S(2)}) async-start(bf16[8,64,768]{2,1,0:T(8,128)(2,1)} %bitcast.101), calls=%async_computation.2 | async-start | bytes 1572864 | tf_op jit(solution)/shard_map/all_to_all | solution.py:759
  156.9 30.3 %collective-permute-start.7 = (bf16[384,1536]{1,0:T(8,128)(2,1)}, bf16[384,1536]{1,0:T(8,128)(2,1)S(1)}, u32[]{:S(2)}, u32[]{:S(2)}) collective-permute-start(bf16[384,1536]{1,0:T(8,128)(2,1)} %shard_map.303), channel_id=1, source_target_pairs={{0,4},{4,0},{8,12},{12,8},{16,20},{20,16},{24,28},{28,24},{1,5},{5... | collective-permute-start | bytes 3538952 | tf_op jit(solution)/shard_map/ppermute | solution.py:609
  191.6 50.4 %all-to-all-start.3 = ((bf16[8,64,768]{2,1,0:T(8,128)(2,1)}), bf16[8,64,768]{2,1,0:T(8,128)(2,1)S(1)}, u32[]{:S(2)}, u32[]{:S(2)}) async-start(bf16[8,64,768]{2,1,0:T(8,128)(2,1)} %shard_map.308), calls=%async_computation.3 | async-start | bytes 1572864 | tf_op jit(solution)/shard_map/all_to_all | solution.py:776
  197.4 42.5 %collective-permute-start.11 = (bf16[768,768]{1,0:T(8,128)(2,1)}, bf16[768,768]{1,0:T(8,128)(2,1)}, u32[]{:S(2)}, u32[]{:S(2)}) collective-permute-start(bf16[768,768]{1,0:T(8,128)(2,1)} %shard_map.305), channel_id=1, source_target_pairs={{0,4},{4,0},{8,12},{12,8},{16,20},{20,16},{24,28},{28,24},{1,5},{5... | collective-permute-start | bytes 3538952 | tf_op jit(solution)/shard_map/ppermute | solution.py:609
  202.9 37.0 %collective-permute-start.10 = (bf16[96,1536]{1,0:T(8,128)(2,1)}, bf16[96,1536]{1,0:T(8,128)(2,1)}, u32[]{:S(2)}, u32[]{:S(2)}) collective-permute-start(bf16[96,1536]{1,0:T(8,128)(2,1)} %get-tuple-element.288), channel_id=1, source_target_pairs={{0,24},{4,28},{8,16},{12,20},{16,8},{20,12},{24,0},{28,4},{1,25},{... | collective-permute-start | bytes 884744 | tf_op jit(solution)/shard_map/ppermute | solution.py:609
  206.2 33.7 %collective-permute-start.8 = (bf16[96,1536]{1,0:T(8,128)(2,1)}, bf16[96,1536]{1,0:T(8,128)(2,1)}, u32[]{:S(2)}, u32[]{:S(2)}) collective-permute-start(bf16[96,1536]{1,0:T(8,128)(2,1)} %get-tuple-element.290), channel_id=1, source_target_pairs={{0,8},{4,12},{8,0},{12,4},{16,24},{20,28},{24,16},{28,20},{1,9},{5... | collective-permute-start | bytes 884744 | tf_op jit(solution)/shard_map/ppermute | solution.py:609
  206.2 35.8 %collective-permute-start.9 = (bf16[96,1536]{1,0:T(8,128)(2,1)S(1)}, bf16[96,1536]{1,0:T(8,128)(2,1)}, u32[]{:S(2)}, u32[]{:S(2)}) collective-permute-start(bf16[96,1536]{1,0:T(8,128)(2,1)S(1)} %get-tuple-element.289), channel_id=1, source_target_pairs={{0,16},{4,20},{8,24},{12,28},{16,0},{20,4},{24,8},{28,12},{1,17},{... | collective-permute-start | bytes 884744 | tf_op jit(solution)/shard_map/ppermute | solution.py:609
  245.9 32.9 %collective-permute-start.15 = (bf16[1536,768]{1,0:T(8,128)(2,1)}, bf16[1536,768]{1,0:T(8,128)(2,1)}, u32[]{:S(2)}, u32[]{:S(2)}) collective-permute-start(bf16[1536,768]{1,0:T(8,128)(2,1)} %shard_map.310), channel_id=1, source_target_pairs={{0,1},{1,0},{2,3},{3,2},{4,5},{5,4},{6,7},{7,6},{8,9},{9,8},{10,11... | collective-permute-start | bytes 7077896 | tf_op jit(solution)/shard_map/ppermute | solution.py:609
  245.9 29.3 %collective-permute-start.13 = (bf16[192,768]{1,0:T(8,128)(2,1)}, bf16[192,768]{1,0:T(8,128)(2,1)S(1)}, u32[]{:S(2)}, u32[]{:S(2)}) collective-permute-start(bf16[192,768]{1,0:T(8,128)(2,1)} %get-tuple-element.286), channel_id=1, source_target_pairs={{0,16},{4,20},{8,24},{12,28},{16,0},{20,4},{24,8},{28,12},{1,17},{... | collective-permute-start | bytes 884744 | tf_op jit(solution)/shard_map/ppermute | solution.py:609
  247.7 31.1 %collective-permute-start.14 = (bf16[192,768]{1,0:T(8,128)(2,1)}, bf16[192,768]{1,0:T(8,128)(2,1)S(1)}, u32[]{:S(2)}, u32[]{:S(2)}) collective-permute-start(bf16[192,768]{1,0:T(8,128)(2,1)} %get-tuple-element.285), channel_id=1, source_target_pairs={{0,24},{4,28},{8,16},{12,20},{16,8},{20,12},{24,0},{28,4},{1,25},{... | collective-permute-start | bytes 884744 | tf_op jit(solution)/shard_map/ppermute | solution.py:609
  281.1 48.5 %collective-permute-start.22 = (bf16[1536,384]{1,0:T(8,128)(2,1)S(1)}, bf16[1536,384]{1,0:T(8,128)(2,1)S(1)}, u32[]{:S(2)}, u32[]{:S(2)}) collective-permute-start(bf16[1536,384]{1,0:T(8,128)(2,1)S(1)} %add_convert_fusion.2), channel_id=1, source_target_pairs={{0,2},{1,3},{2,0},{3,1},{4,6},{5,7},{6,4},{7,5},{8,10},{9,11},{10,... | collective-permute-start | bytes 3538952 | tf_op jit(solution)/shard_map/ppermute | solution.py:609
  297.0 54.5 %collective-permute-start.23 = (bf16[768,768]{1,0:T(8,128)(2,1)}, bf16[768,768]{1,0:T(8,128)(2,1)S(1)}, u32[]{:S(2)}, u32[]{:S(2)}) collective-permute-start(bf16[768,768]{1,0:T(8,128)(2,1)} %shard_map.314), channel_id=1, source_target_pairs={{0,4},{4,0},{8,12},{12,8},{16,20},{20,16},{24,28},{28,24},{1,5},{5... | collective-permute-start | bytes 3538952 | tf_op jit(solution)/shard_map/ppermute | solution.py:609
  297.0 29.5 %collective-permute-start.18 = (f32[1,384,256]{2,1,0:T(8,128)}, f32[1,384,256]{2,1,0:T(8,128)}, u32[]{:S(2)}, u32[]{:S(2)}) collective-permute-start(f32[1,384,256]{2,1,0:T(8,128)} %slice_add_fusion), channel_id=1, source_target_pairs={{0,2},{1,3},{2,0},{3,1},{4,6},{5,7},{6,4},{7,5},{8,10},{9,11},{10,... | collective-permute-start | bytes 1179656 | tf_op jit(solution)/shard_map/ppermute | solution.py:609
  321.0 30.4 %collective-permute-start.24 = (bf16[192,768]{1,0:T(8,128)(2,1)}, bf16[192,768]{1,0:T(8,128)(2,1)}, u32[]{:S(2)}, u32[]{:S(2)}) collective-permute-start(bf16[192,768]{1,0:T(8,128)(2,1)} %get-tuple-element.259), channel_id=1, source_target_pairs={{0,8},{4,12},{8,0},{12,4},{16,24},{20,28},{24,16},{28,20},{1,9},{5... | collective-permute-start | bytes 884744 | tf_op jit(solution)/shard_map/ppermute | solution.py:609
  321.0 30.4 %collective-permute-start.25 = (bf16[192,768]{1,0:T(8,128)(2,1)}, bf16[192,768]{1,0:T(8,128)(2,1)}, u32[]{:S(2)}, u32[]{:S(2)}) collective-permute-start(bf16[192,768]{1,0:T(8,128)(2,1)} %get-tuple-element.259), channel_id=1, source_target_pairs={{0,16},{4,20},{8,24},{12,28},{16,0},{20,4},{24,8},{28,12},{1,17},{... | collective-permute-start | bytes 884744 | tf_op jit(solution)/shard_map/ppermute | solution.py:609
  383.9 30.1 %collective-permute-start.34 = (bf16[384,1536]{1,0:T(8,128)(2,1)}, bf16[384,1536]{1,0:T(8,128)(2,1)}, u32[]{:S(2)}, u32[]{:S(2)}) collective-permute-start(bf16[384,1536]{1,0:T(8,128)(2,1)} %copy-done.11), channel_id=1, source_target_pairs={{0,4},{4,0},{8,12},{12,8},{16,20},{20,16},{24,28},{28,24},{1,5},{5... | collective-permute-start | bytes 3538952 | tf_op jit(solution)/shard_map/ppermute | solution.py:609
  402.1 64.2 %collective-permute-start.42 = (bf16[768,768]{1,0:T(8,128)(2,1)}, bf16[768,768]{1,0:T(8,128)(2,1)}, u32[]{:S(2)}, u32[]{:S(2)}) collective-permute-start(bf16[768,768]{1,0:T(8,128)(2,1)} %constant_dynamic-update-slice_fusion.5), channel_id=1, source_target_pairs={{0,4},{4,0},{8,12},{12,8},{16,20},{20,16},{24,28},{28,24},{1,5},{5... | collective-permute-start | bytes 3538952 | tf_op jit(solution)/shard_map/ppermute | solution.py:609
  423.8 42.5 %collective-permute-start.39 = (bf16[192,768]{1,0:T(8,128)(2,1)}, bf16[192,768]{1,0:T(8,128)(2,1)}, u32[]{:S(2)}, u32[]{:S(2)}) collective-permute-start(bf16[192,768]{1,0:T(8,128)(2,1)} %get-tuple-element.257), channel_id=1, source_target_pairs={{0,8},{4,12},{8,0},{12,4},{16,24},{20,28},{24,16},{28,20},{1,9},{5... | collective-permute-start | bytes 884744 | tf_op jit(solution)/shard_map/ppermute | solution.py:609
  424.4 41.9 %collective-permute-start.40 = (bf16[192,768]{1,0:T(8,128)(2,1)}, bf16[192,768]{1,0:T(8,128)(2,1)}, u32[]{:S(2)}, u32[]{:S(2)}) collective-permute-start(bf16[192,768]{1,0:T(8,128)(2,1)} %get-tuple-element.257), channel_id=1, source_target_pairs={{0,16},{4,20},{8,24},{12,28},{16,0},{20,4},{24,8},{28,12},{1,17},{... | collective-permute-start | bytes 884744 | tf_op jit(solution)/shard_map/ppermute | solution.py:609
  426.8 39.5 %collective-permute-start.41 = (bf16[192,768]{1,0:T(8,128)(2,1)}, bf16[192,768]{1,0:T(8,128)(2,1)}, u32[]{:S(2)}, u32[]{:S(2)}) collective-permute-start(bf16[192,768]{1,0:T(8,128)(2,1)} %get-tuple-element.257), channel_id=1, source_target_pairs={{0,24},{4,28},{8,16},{12,20},{16,8},{20,12},{24,0},{28,4},{1,25},{... | collective-permute-start | bytes 884744 | tf_op jit(solution)/shard_map/ppermute | solution.py:609
  429.4 44.0 %all-to-all-start.4 = ((f32[8,24,768]{2,1,0:T(8,128)}), f32[8,24,768]{2,1,0:T(8,128)}, u32[]{:S(2)}, u32[]{:S(2)}) async-start(f32[8,24,768]{2,1,0:T(8,128)} %bitcast.34), calls=%async_computation.4 | async-start | bytes 1179648 | tf_op jit(solution)/shard_map/all_to_all | solution.py:1178
  471.4 31.1 %collective-permute-start.43 = (bf16[768,768]{1,0:T(8,128)(2,1)}, bf16[768,768]{1,0:T(8,128)(2,1)S(1)}, u32[]{:S(2)}, u32[]{:S(2)}) collective-permute-start(bf16[768,768]{1,0:T(8,128)(2,1)} %constant_dynamic-update-slice_fusion), channel_id=1, source_target_pairs={{0,4},{4,0},{8,12},{12,8},{16,20},{20,16},{24,28},{28,24},{1,5},{5... | collective-permute-start | bytes 3538952 | tf_op jit(solution)/shard_map/ppermute | solution.py:609
  (86 other events, 868.0 us)
